TPU v7x, 128 devices: a whole 4x4x4 slice. The times are simulated.
128 devices in a mesh: tm: 8 (over y, core), sx: 4 (over z), sy: 4 (over x).
Axes of the slice: x: 4, y: 4, z: 4, core: 2. Of those that a mesh axis runs over, the one named last changes fastest.
Arguments:
- initial: float32 [512, 1536], P('sx', 'sy'), may hold values from -6 to 6
- guesses: float32 [8, 512, 1536], P('tm', 'sx', 'sy'), may hold values from -6 to 6
- conduct: float32 [512, 1536], P('sx', 'sy'), may hold values from 0.25 to 4
- source: float32 [512, 1536], P('sx', 'sy'), may hold values from -6 to 6
Outputs:
- corrected: float32 [8, 512, 1536], P('tm', 'sx', 'sy')
All inputs are finite; a program needn't handle non-finite values.
Results may differ from a plain program's by a relative error of at most 0.00002.
Values sent between devices are 32-bit elements; how exact they have to be, the bound alone decides.
A program may use at most 128 MiB of HBM per device.

v0:
```python
import jax
import jax.numpy as jnp
from jax import lax
from jax.sharding import PartitionSpec as P

FINE = 4


TIME_STEP = 0.035
NONLINEAR_GAIN = 0.5


def with_halo(cells, sides, width):
    for axis, dim in sides:
        count = lax.axis_size(axis)
        ends = count - 1
        head = lax.slice_in_dim(cells, 0, width, axis=dim)
        tail = lax.slice_in_dim(cells, cells.shape[dim] - width, cells.shape[dim], axis=dim)
        cells = jnp.concatenate(
            [
                lax.ppermute(tail, axis, [(i, (i + 1) % count) for i in range(ends)]),
                cells,
                lax.ppermute(head, axis, [((i + 1) % count, i) for i in range(ends)]),
            ],
            axis=dim,
        )
    return cells


def from_behind(block, axis, distance):
    devices = range(lax.axis_size(axis))
    route = [(i - distance, i) for i in devices if i - distance in devices]
    return lax.ppermute(block, axis, route)


def conductance(values, factor):
    return factor * (1.0 + NONLINEAR_GAIN * jnp.tanh(values))


def divergence(v_ext, c_ext, source, inv_area):
    k_ext = conductance(v_ext, c_ext)
    centre = v_ext[..., 1:-1, 1:-1]
    k_mid = k_ext[..., 1:-1, 1:-1]
    accrued = 0.5 * (k_mid + k_ext[..., 2:, 1:-1]) * (v_ext[..., 2:, 1:-1] - centre)
    accrued = accrued + 0.5 * (k_mid + k_ext[..., :-2, 1:-1]) * (v_ext[..., :-2, 1:-1] - centre)
    accrued = accrued + 0.5 * (k_mid + k_ext[..., 1:-1, 2:]) * (v_ext[..., 1:-1, 2:] - centre)
    accrued = accrued + 0.5 * (k_mid + k_ext[..., 1:-1, :-2]) * (v_ext[..., 1:-1, :-2] - centre)
    return accrued * inv_area + source


def restrict(field_in):
    leading = field_in.shape[:-2]
    height, breadth = (field_in.shape[-2], field_in.shape[-1])
    blocks = field_in.reshape(leading + (height // 2, 2, breadth // 2, 2))
    return 0.25 * (
        blocks[..., :, 0, :, 0]
        + blocks[..., :, 0, :, 1]
        + blocks[..., :, 1, :, 0]
        + blocks[..., :, 1, :, 1]
    )


def prolong(field_in):
    return jnp.repeat(jnp.repeat(field_in, 2, axis=-2), 2, axis=-1)


def crop_rim(field_in, outer, margin):
    height = field_in.shape[-2] - 2 * outer
    breadth = field_in.shape[-1] - 2 * outer
    first = outer - margin
    return field_in[..., first : first + height + 2 * margin, first : first + breadth + 2 * margin]


def single_advance(present, coefficients, inv_area, step_len):
    conduct_one = coefficients[0, 1:-1, 1:-1]
    source_in = coefficients[1, 2:-2, 2:-2]
    padded = with_halo(present, (("sx", 1), ("sy", 2)), 1)
    slope_one = divergence(padded, conduct_one, source_in, inv_area)
    section_value = present + step_len * slope_one
    section_ext = with_halo(section_value, (("sx", 1), ("sy", 2)), 1)
    slope_two = divergence(section_ext, conduct_one, source_in, inv_area)
    return 0.5 * (present + section_value + step_len * slope_two)


def local(initial, guesses, conduct, source):
    outer = 2 * FINE
    leading_slab = lax.axis_index("tm") == 0
    coefficients = with_halo(jnp.stack([conduct, source]), (("sx", 1), ("sy", 2)), outer)
    fine_coef = crop_rim(coefficients, outer, 2)
    coarse_coef = crop_rim(restrict(coefficients), outer // 2, 2)

    def fine_run(states):
        for repeat_index in range(FINE):
            states = single_advance(states, fine_coef, 1.0, TIME_STEP)
        return states

    def coarse_step(states):
        return single_advance(states, coarse_coef, 0.25, TIME_STEP * FINE)

    def earlier(values):
        prior = from_behind(values[-1], "tm", 1)
        prior = jnp.where(leading_slab, initial, prior)
        return jnp.concatenate([prior[None], values[:-1]], axis=0)

    relaxed = fine_run(earlier(guesses))
    again = earlier(relaxed)
    propagated = fine_run(again)
    targets = restrict(propagated) - coarse_step(restrict(again))
    anchor = restrict(initial)

    def one_round(round_index, carried):
        incoming = from_behind(carried[-1], "tm", 1)
        current = jnp.where(leading_slab, anchor, incoming)
        current = coarse_step(current[None])[0] + targets[0]
        series = [current]
        return jnp.stack(series)

    coarse = lax.fori_loop(0, lax.axis_size("tm"), one_round, jnp.zeros_like(targets))
    return relaxed + prolong(coarse - restrict(relaxed))


def solution(mesh):
    in_specs = (P("sx", "sy"), P("tm", "sx", "sy"), P("sx", "sy"), P("sx", "sy"))
    out_specs = P("tm", "sx", "sy")
    return jax.shard_map(local, mesh=mesh, in_specs=in_specs, out_specs=out_specs, check_vma=False)
```

profile of v0, /device:TPU:112, one launch (start us, length us, event | category | flops | bytes accessed | tf_op | source)
XLA Modules:
  0.0 833.4 jit_solution(13597979853060067823)
XLA Ops:
  6.6 4.6 collective-permute-start.11
  13.7 4.6 collective-permute-start.15
  25.4 4.5 collective-permute-start.16
  37.7 5.0 collective-permute-start.19
  57.1 5.0 collective-permute-start.23
  76.3 5.0 collective-permute-start.27
  94.2 5.0 collective-permute-start.31
  112.2 5.0 collective-permute-start.35
  130.1 5.0 collective-permute-start.39
  148.1 5.0 collective-permute-start.43
  166.5 5.1 collective-permute-done.46
  173.0 5.0 collective-permute-start.48
  186.7 14.5 %reshape.1150 = f32[64,2,192,2]{3,2,1,0:T(8,128)} reshape(f32[128,384]{1,0:T(8,128)S(1)} %copy-done) | data formatting | bytes 393216 | tf_op jit(solution)/shard_map/reshape | solution.py:54
  203.5 5.0 collective-permute-start.52
  208.5 11.1 %fusion.49 = f32[64,192]{1,0:T(8,128)S(1)} fusion(f32[64,2,192,2]{3,2,1,0:T(8,128)} %reshape.1150), kind=kLoop, calls=%fused_computation.83 | loop fusion | flops 49152 | bytes 245760 | tf_op jit(solution)/shard_map/mul | solution.py:55
  219.9 13.9 %reshape.1151 = f32[2,72,2,200,2]{4,3,2,1,0:T(8,128)} reshape(f32[2,144,400]{2,1,0:T(8,128)S(1)} %copy.48) | data formatting | bytes 921600 | tf_op jit(solution)/shard_map/reshape | solution.py:54
  233.9 4.5 collective-permute-start.53
  239.7 21.5 %fusion.47 = f32[2,72,200]{2,1,0:T(8,128)S(1)} fusion(f32[2,72,2,200,2]{4,3,2,1,0:T(8,128)} %reshape.1151), kind=kLoop, calls=%fused_computation.78 | loop fusion | flops 115200 | bytes 576000 | tf_op jit(solution)/shard_map/mul | solution.py:55
  261.4 13.9 %reshape.1156 = f32[1,64,2,192,2]{2,1,4,3,0:T(8,128)} reshape(f32[1,128,384]{1,2,0:T(8,128)S(1)} %fusion.252) | data formatting | bytes 393216 | tf_op jit(solution)/shard_map/reshape | solution.py:54
  277.6 4.6 collective-permute-start.56
  282.2 16.7 %fusion.445 = (f32[1,64,1,192,1]{2,1,4,3,0:T(8,128)}, f32[1,64,1,192,1]{2,1,4,3,0:T(8,128)}, f32[1,64,1,192,1]{2,1,4,3,0:T(8,128)}, f32[1,64,1,192,1]{2,1,4,3,0:T(8,128)}) fusion(f32[1,64,2,192,2]{2,1,4,3,0:T(8,128)} %reshape.1156), kind=kLoop, calls=%fused_computation.776 | loop fusion | bytes 393216 | tf_op jit(solution)/shard_map/slice | solution.py:57
  298.8 5.0 copy.81
  303.8 5.0 copy.82
  308.8 5.0 copy.83
  313.8 5.0 copy.84
  318.8 13.9 %reshape.1155 = f32[1,64,2,192,2]{2,1,4,3,0:T(8,128)} reshape(f32[128,384]{0,1:T(8,128)S(1)} %broadcast_select_fusion) | data formatting | bytes 393216 | tf_op jit(solution)/shard_map/reshape;broadcast_in_dim | solution.py:54
  332.8 4.5 collective-permute-start.57
  339.0 16.7 %fusion.447 = (f32[1,64,1,192,1]{2,1,4,3,0:T(8,128)}, f32[1,64,1,192,1]{2,1,4,3,0:T(8,128)}, f32[1,64,1,192,1]{2,1,4,3,0:T(8,128)}, f32[1,64,1,192,1]{2,1,4,3,0:T(8,128)}) fusion(f32[1,64,2,192,2]{2,1,4,3,0:T(8,128)} %reshape.1155), kind=kLoop, calls=%fused_computation.778 | loop fusion | bytes 393216 | tf_op jit(solution)/shard_map/slice | solution.py:57
  355.7 5.0 copy.77
  360.7 5.0 copy.78
  365.7 5.0 copy.79
  370.6 5.0 copy.80
  377.9 4.6 collective-permute-start.60
  392.9 5.0 collective-permute-start.80
  400.3 4.6 collective-permute-start.64
  414.0 4.5 collective-permute-start.81
  422.1 5.0 collective-permute-start.68
  442.7 5.0 collective-permute-start.72
  449.1 4.5 collective-permute-start.84
  463.4 4.6 collective-permute-start.76
  471.4 4.7 collective-permute-start.77
  482.5 13.9 %reshape.1154 = f32[1,64,2,192,2]{2,1,4,3,0:T(8,128)} reshape(f32[1,128,384]{1,2,0:T(8,128)S(1)} %fusion.104) | data formatting | bytes 393216 | tf_op jit(solution)/shard_map/reshape | solution.py:54
  496.4 16.7 %fusion.446 = (f32[1,64,1,192,1]{2,1,4,3,0:T(8,128)}, f32[1,64,1,192,1]{2,1,4,3,0:T(8,128)}, f32[1,64,1,192,1]{2,1,4,3,0:T(8,128)}, f32[1,64,1,192,1]{2,1,4,3,0:T(8,128)}) fusion(f32[1,64,2,192,2]{2,1,4,3,0:T(8,128)} %reshape.1154), kind=kLoop, calls=%fused_computation.777 | loop fusion | bytes 393216 | tf_op jit(solution)/shard_map/slice | solution.py:57
  513.1 5.0 copy.73
  518.0 5.0 copy.74
  523.0 5.0 copy.75
  528.0 5.0 copy.76
  533.2 298.8 %while.11 = (s32[]{:T(128)}, f32[1,64,192]{2,1,0:T(8,128)S(1)}, pred[]{:T(512)}, f32[64,192]{1,0:T(8,128)S(1)}, f32[2,68,196]{2,1,0:T(8,128)S(1)}, /*index=5*/f32[1,64,192]{2,1,0:T(8,128)S(1)}, s32[]{:T(128)}, s32[]{:T(128)}) while((s32[]{:T(128)}, f32[1,64,192]{2,1,0:T(8,128)S(1)}, pred[]{:T(512)}, f32[64,192]{1,0:T(8,128)S(1)}, ...), condition=%wide.region_1.2_spmd.clone, body=%wide.region_0.1_spmd.clone.sunk | while | flops 1053243 | bytes 1866504 | solution.py:118
  (467 shorter events, 497.8 us)
Async XLA Ops:
  1.1 11.2 %collective-permute-start.9 = (f32[128,384]{0,1:T(8,128)S(1)}, f32[128,384]{0,1:T(8,128)S(1)}, u32[]{:S(2)}, u32[]{:S(2)}) collective-permute-start(f32[128,384]{0,1:T(8,128)S(1)} %bitcast.61), channel_id=1, source_target_pairs={{0,16},{16,32},{32,48},{48,64},{64,80},{80,96},{96,112},{1,17},{17... | collective-permute-start | bytes 589832 | tf_op jit(solution)/shard_map/ppermute | solution.py:33
  5.3 13.5 %collective-permute-start.10 = (f32[2,8,384]{1,2,0:T(8,128)S(1)}, f32[2,8,384]{1,2,0:T(8,128)S(1)}, u32[]{:S(2)}, u32[]{:S(2)}) collective-permute-start(f32[2,8,384]{1,2,0:T(8,128)S(1)} %get-tuple-element.125), channel_id=1, source_target_pairs={{0,4},{4,8},{8,12},{1,5},{5,9},{9,13},{2,6},{6,10},{10,14},{3,7},{... | collective-permute-start | bytes 73736 | tf_op jit(solution)/shard_map/ppermute | solution.py:21
  6.6 13.9 %collective-permute-start.11 = (f32[2,8,384]{1,2,0:T(8,128)S(1)}, f32[2,8,384]{1,2,0:T(8,128)S(1)}, u32[]{:S(2)}, u32[]{:S(2)}) collective-permute-start(f32[2,8,384]{1,2,0:T(8,128)S(1)} %get-tuple-element.126), channel_id=1, source_target_pairs={{4,0},{8,4},{12,8},{5,1},{9,5},{13,9},{6,2},{10,6},{14,10},{7,3},{... | collective-permute-start | bytes 73736 | tf_op jit(solution)/shard_map/ppermute | solution.py:23
  12.4 12.9 %collective-permute-start.14 = (f32[1,1,384]{1,2,0:T(8,128)S(1)}, f32[1,1,384]{1,2,0:T(8,128)S(1)}, u32[]{:S(2)}, u32[]{:S(2)}) collective-permute-start(f32[1,1,384]{1,2,0:T(8,128)S(1)} %get-tuple-element.157), channel_id=1, source_target_pairs={{0,4},{4,8},{8,12},{1,5},{5,9},{9,13},{2,6},{6,10},{10,14},{3,7},{... | collective-permute-start | bytes 4616 | tf_op jit(solution)/shard_map/ppermute | solution.py:21
  13.7 11.6 %collective-permute-start.15 = (f32[1,1,384]{1,2,0:T(8,128)S(1)}, f32[1,1,384]{1,2,0:T(8,128)S(1)}, u32[]{:S(2)}, u32[]{:S(2)}) collective-permute-start(f32[1,1,384]{1,2,0:T(8,128)S(1)} %get-tuple-element.158), channel_id=1, source_target_pairs={{4,0},{8,4},{12,8},{5,1},{9,5},{13,9},{6,2},{10,6},{14,10},{7,3},{... | collective-permute-start | bytes 4616 | tf_op jit(solution)/shard_map/ppermute | solution.py:23
  20.6 10.7 %collective-permute-start.12 = (f32[2,144,8]{1,2,0:T(8,128)S(1)}, f32[2,144,8]{1,2,0:T(8,128)S(1)}, u32[]{:S(2)}, u32[]{:S(2)}) collective-permute-start(f32[2,144,8]{1,2,0:T(8,128)S(1)} %get-tuple-element.91), channel_id=1, source_target_pairs={{0,1},{1,2},{2,3},{4,5},{5,6},{6,7},{8,9},{9,10},{10,11},{12,13},{... | collective-permute-start | bytes 27656 | tf_op jit(solution)/shard_map/ppermute | solution.py:21
  36.4 8.0 collective-permute-start.18
  37.7 8.2 collective-permute-start.19
  55.8 8.0 collective-permute-start.22
  57.1 8.2 collective-permute-start.23
  75.0 8.0 collective-permute-start.26
  76.3 8.2 collective-permute-start.27
  92.9 8.0 collective-permute-start.30
  94.2 8.2 collective-permute-start.31
  110.9 8.0 collective-permute-start.34
  112.2 8.2 collective-permute-start.35
  128.8 8.0 collective-permute-start.38
  130.1 8.3 %collective-permute-start.39 = (f32[1,1,384]{1,2,0:T(8,128)S(1)}, f32[1,1,384]{1,2,0:T(8,128)S(1)}, u32[]{:S(2)}, u32[]{:S(2)}) collective-permute-start(f32[1,1,384]{1,2,0:T(8,128)S(1)} %get-tuple-element.146), channel_id=1, source_target_pairs={{4,0},{8,4},{12,8},{5,1},{9,5},{13,9},{6,2},{10,6},{14,10},{7,3},{... | collective-permute-start | bytes 4616 | tf_op jit(solution)/shard_map/ppermute | solution.py:23
  146.8 8.0 collective-permute-start.42
  148.1 8.2 collective-permute-start.43
  171.7 9.9 %collective-permute-start.47 = (f32[1,1,384]{1,2,0:T(8,128)S(1)}, f32[1,1,384]{1,2,0:T(8,128)S(1)}, u32[]{:S(2)}, u32[]{:S(2)}) collective-permute-start(f32[1,1,384]{1,2,0:T(8,128)S(1)} %get-tuple-element.141), channel_id=1, source_target_pairs={{0,4},{4,8},{8,12},{1,5},{5,9},{9,13},{2,6},{6,10},{10,14},{3,7},{... | collective-permute-start | bytes 4616 | tf_op jit(solution)/shard_map/ppermute | solution.py:21
  173.0 10.2 %collective-permute-start.48 = (f32[1,1,384]{1,2,0:T(8,128)S(1)}, f32[1,1,384]{1,2,0:T(8,128)S(1)}, u32[]{:S(2)}, u32[]{:S(2)}) collective-permute-start(f32[1,1,384]{1,2,0:T(8,128)S(1)} %get-tuple-element.142), channel_id=1, source_target_pairs={{4,0},{8,4},{12,8},{5,1},{9,5},{13,9},{6,2},{10,6},{14,10},{7,3},{... | collective-permute-start | bytes 4616 | tf_op jit(solution)/shard_map/ppermute | solution.py:23
  183.3 17.9 %collective-permute-start.49 = (f32[1,130,1]{1,2,0:T(1,128)S(1)}, f32[1,130,1]{1,2,0:T(1,128)S(1)}, u32[]{:S(2)}, u32[]{:S(2)}) collective-permute-start(f32[1,130,1]{1,2,0:T(1,128)S(1)} %get-tuple-element.108), channel_id=1, source_target_pairs={{0,1},{1,2},{2,3},{4,5},{5,6},{6,7},{8,9},{9,10},{10,11},{12,13},{... | collective-permute-start | bytes 1568 | tf_op jit(solution)/shard_map/ppermute | solution.py:21
  185.3 16.0 %collective-permute-start.50 = (f32[1,130,1]{1,2,0:T(1,128)S(1)}, f32[1,130,1]{1,2,0:T(1,128)S(1)}, u32[]{:S(2)}, u32[]{:S(2)}) collective-permute-start(f32[1,130,1]{1,2,0:T(1,128)S(1)} %get-tuple-element.107), channel_id=1, source_target_pairs={{1,0},{2,1},{3,2},{5,4},{6,5},{7,6},{9,8},{10,9},{11,10},{13,12},{... | collective-permute-start | bytes 1568 | tf_op jit(solution)/shard_map/ppermute | solution.py:23
  202.2 31.6 %collective-permute-start.51 = (f32[1,1,384]{1,2,0:T(8,128)S(1)}, f32[1,1,384]{1,2,0:T(8,128)S(1)}, u32[]{:S(2)}, u32[]{:S(2)}) collective-permute-start(f32[1,1,384]{1,2,0:T(8,128)S(1)} %get-tuple-element.139), channel_id=1, source_target_pairs={{0,4},{4,8},{8,12},{1,5},{5,9},{9,13},{2,6},{6,10},{10,14},{3,7},{... | collective-permute-start | bytes 4616 | tf_op jit(solution)/shard_map/ppermute | solution.py:21
  203.5 30.3 %collective-permute-start.52 = (f32[1,1,384]{1,2,0:T(8,128)S(1)}, f32[1,1,384]{1,2,0:T(8,128)S(1)}, u32[]{:S(2)}, u32[]{:S(2)}) collective-permute-start(f32[1,1,384]{1,2,0:T(8,128)S(1)} %get-tuple-element.140), channel_id=1, source_target_pairs={{4,0},{8,4},{12,8},{5,1},{9,5},{13,9},{6,2},{10,6},{14,10},{7,3},{... | collective-permute-start | bytes 4616 | tf_op jit(solution)/shard_map/ppermute | solution.py:23
  233.9 41.4 %collective-permute-start.53 = (f32[1,130,1]{1,2,0:T(1,128)S(1)}, f32[1,130,1]{1,2,0:T(1,128)S(1)}, u32[]{:S(2)}, u32[]{:S(2)}) collective-permute-start(f32[1,130,1]{1,2,0:T(1,128)S(1)} %get-tuple-element.106), channel_id=1, source_target_pairs={{0,1},{1,2},{2,3},{4,5},{5,6},{6,7},{8,9},{9,10},{10,11},{12,13},{... | collective-permute-start | bytes 1568 | tf_op jit(solution)/shard_map/ppermute | solution.py:21
  238.4 36.9 %collective-permute-start.54 = (f32[1,130,1]{1,2,0:T(1,128)S(1)}, f32[1,130,1]{1,2,0:T(1,128)S(1)}, u32[]{:S(2)}, u32[]{:S(2)}) collective-permute-start(f32[1,130,1]{1,2,0:T(1,128)S(1)} %get-tuple-element.105), channel_id=1, source_target_pairs={{1,0},{2,1},{3,2},{5,4},{6,5},{7,6},{9,8},{10,9},{11,10},{13,12},{... | collective-permute-start | bytes 1568 | tf_op jit(solution)/shard_map/ppermute | solution.py:23
  276.3 56.4 %collective-permute-start.55 = (f32[1,1,384]{1,2,0:T(8,128)S(1)}, f32[1,1,384]{1,2,0:T(8,128)S(1)}, u32[]{:S(2)}, u32[]{:S(2)}) collective-permute-start(f32[1,1,384]{1,2,0:T(8,128)S(1)} %get-tuple-element.137), channel_id=1, source_target_pairs={{0,4},{4,8},{8,12},{1,5},{5,9},{9,13},{2,6},{6,10},{10,14},{3,7},{... | collective-permute-start | bytes 4616 | tf_op jit(solution)/shard_map/ppermute | solution.py:21
  277.6 55.1 %collective-permute-start.56 = (f32[1,1,384]{1,2,0:T(8,128)S(1)}, f32[1,1,384]{1,2,0:T(8,128)S(1)}, u32[]{:S(2)}, u32[]{:S(2)}) collective-permute-start(f32[1,1,384]{1,2,0:T(8,128)S(1)} %get-tuple-element.138), channel_id=1, source_target_pairs={{4,0},{8,4},{12,8},{5,1},{9,5},{13,9},{6,2},{10,6},{14,10},{7,3},{... | collective-permute-start | bytes 4616 | tf_op jit(solution)/shard_map/ppermute | solution.py:23
  332.8 42.9 %collective-permute-start.57 = (f32[1,130,1]{1,2,0:T(1,128)S(1)}, f32[1,130,1]{1,2,0:T(1,128)S(1)}, u32[]{:S(2)}, u32[]{:S(2)}) collective-permute-start(f32[1,130,1]{1,2,0:T(1,128)S(1)} %get-tuple-element.104), channel_id=1, source_target_pairs={{0,1},{1,2},{2,3},{4,5},{5,6},{6,7},{8,9},{9,10},{10,11},{12,13},{... | collective-permute-start | bytes 1568 | tf_op jit(solution)/shard_map/ppermute | solution.py:21
  337.3 38.3 %collective-permute-start.58 = (f32[1,130,1]{1,2,0:T(1,128)S(1)}, f32[1,130,1]{1,2,0:T(1,128)S(1)}, u32[]{:S(2)}, u32[]{:S(2)}) collective-permute-start(f32[1,130,1]{1,2,0:T(1,128)S(1)} %get-tuple-element.103), channel_id=1, source_target_pairs={{1,0},{2,1},{3,2},{5,4},{6,5},{7,6},{9,8},{10,9},{11,10},{13,12},{... | collective-permute-start | bytes 1568 | tf_op jit(solution)/shard_map/ppermute | solution.py:23
  385.7 12.2 %collective-permute-start.61 = (f32[1,130,1]{1,2,0:T(1,128)S(1)}, f32[1,130,1]{1,2,0:T(1,128)S(1)}, u32[]{:S(2)}, u32[]{:S(2)}) collective-permute-start(f32[1,130,1]{1,2,0:T(1,128)S(1)} %get-tuple-element.102), channel_id=1, source_target_pairs={{0,1},{1,2},{2,3},{4,5},{5,6},{6,7},{8,9},{9,10},{10,11},{12,13},{... | collective-permute-start | bytes 1568 | tf_op jit(solution)/shard_map/ppermute | solution.py:21
  391.6 13.2 %collective-permute-start.79 = (f32[1,1,192]{2,1,0:T(1,128)S(1)}, f32[1,1,192]{2,1,0:T(1,128)S(1)}, u32[]{:S(2)}, u32[]{:S(2)}) collective-permute-start(f32[1,1,192]{2,1,0:T(1,128)S(1)} %get-tuple-element.165), channel_id=1, source_target_pairs={{0,4},{4,8},{8,12},{1,5},{5,9},{9,13},{2,6},{6,10},{10,14},{3,7},{... | collective-permute-start | bytes 2312 | tf_op jit(solution)/shard_map/ppermute | solution.py:21
  392.9 11.9 %collective-permute-start.80 = (f32[1,1,192]{2,1,0:T(1,128)S(1)}, f32[1,1,192]{2,1,0:T(1,128)S(1)}, u32[]{:S(2)}, u32[]{:S(2)}) collective-permute-start(f32[1,1,192]{2,1,0:T(1,128)S(1)} %get-tuple-element.166), channel_id=1, source_target_pairs={{4,0},{8,4},{12,8},{5,1},{9,5},{13,9},{6,2},{10,6},{14,10},{7,3},{... | collective-permute-start | bytes 2312 | tf_op jit(solution)/shard_map/ppermute | solution.py:23
  400.3 7.7 collective-permute-start.64
  408.1 11.8 %collective-permute-start.65 = (f32[1,130,1]{1,2,0:T(1,128)S(1)}, f32[1,130,1]{1,2,0:T(1,128)S(1)}, u32[]{:S(2)}, u32[]{:S(2)}) collective-permute-start(f32[1,130,1]{1,2,0:T(1,128)S(1)} %get-tuple-element.100), channel_id=1, source_target_pairs={{0,1},{1,2},{2,3},{4,5},{5,6},{6,7},{8,9},{9,10},{10,11},{12,13},{... | collective-permute-start | bytes 1568 | tf_op jit(solution)/shard_map/ppermute | solution.py:21
  414.0 13.2 %collective-permute-start.81 = (f32[1,66,1]{2,1,0:T(8,128)S(1)}, f32[1,66,1]{2,1,0:T(8,128)S(1)}, u32[]{:S(2)}, u32[]{:S(2)}) collective-permute-start(f32[1,66,1]{2,1,0:T(8,128)S(1)} %get-tuple-element.162), channel_id=1, source_target_pairs={{0,1},{1,2},{2,3},{4,5},{5,6},{6,7},{8,9},{9,10},{10,11},{12,13},{... | collective-permute-start | bytes 800 | tf_op jit(solution)/shard_map/ppermute | solution.py:21
  418.5 8.7 %collective-permute-start.82 = (f32[1,66,1]{2,1,0:T(8,128)S(1)}, f32[1,66,1]{2,1,0:T(8,128)S(1)}, u32[]{:S(2)}, u32[]{:S(2)}) collective-permute-start(f32[1,66,1]{2,1,0:T(8,128)S(1)} %get-tuple-element.161), channel_id=1, source_target_pairs={{1,0},{2,1},{3,2},{5,4},{6,5},{7,6},{9,8},{10,9},{11,10},{13,12},{... | collective-permute-start | bytes 800 | tf_op jit(solution)/shard_map/ppermute | solution.py:23
  420.8 8.0 collective-permute-start.67
  422.1 8.2 collective-permute-start.68
  441.4 12.2 %collective-permute-start.71 = (f32[1,1,384]{1,2,0:T(8,128)S(1)}, f32[1,1,384]{1,2,0:T(8,128)S(1)}, u32[]{:S(2)}, u32[]{:S(2)}) collective-permute-start(f32[1,1,384]{1,2,0:T(8,128)S(1)} %get-tuple-element.129), channel_id=1, source_target_pairs={{0,4},{4,8},{8,12},{1,5},{5,9},{9,13},{2,6},{6,10},{10,14},{3,7},{... | collective-permute-start | bytes 4616 | tf_op jit(solution)/shard_map/ppermute | solution.py:21
  442.7 10.9 %collective-permute-start.72 = (f32[1,1,384]{1,2,0:T(8,128)S(1)}, f32[1,1,384]{1,2,0:T(8,128)S(1)}, u32[]{:S(2)}, u32[]{:S(2)}) collective-permute-start(f32[1,1,384]{1,2,0:T(8,128)S(1)} %get-tuple-element.130), channel_id=1, source_target_pairs={{4,0},{8,4},{12,8},{5,1},{9,5},{13,9},{6,2},{10,6},{14,10},{7,3},{... | collective-permute-start | bytes 4616 | tf_op jit(solution)/shard_map/ppermute | solution.py:23
  447.8 9.2 %collective-permute-start.83 = (f32[1,1,192]{2,1,0:T(1,128)S(1)}, f32[1,1,192]{2,1,0:T(1,128)S(1)}, u32[]{:S(2)}, u32[]{:S(2)}) collective-permute-start(f32[1,1,192]{2,1,0:T(1,128)S(1)} %get-tuple-element.163), channel_id=1, source_target_pairs={{0,4},{4,8},{8,12},{1,5},{5,9},{9,13},{2,6},{6,10},{10,14},{3,7},{... | collective-permute-start | bytes 2312 | tf_op jit(solution)/shard_map/ppermute | solution.py:21
  449.1 7.9 collective-permute-start.84
  462.1 9.2 %collective-permute-start.75 = (f32[1,1,384]{1,2,0:T(8,128)S(1)}, f32[1,1,384]{1,2,0:T(8,128)S(1)}, u32[]{:S(2)}, u32[]{:S(2)}) collective-permute-start(f32[1,1,384]{1,2,0:T(8,128)S(1)} %get-tuple-element.127), channel_id=1, source_target_pairs={{0,4},{4,8},{8,12},{1,5},{5,9},{9,13},{2,6},{6,10},{10,14},{3,7},{... | collective-permute-start | bytes 4616 | tf_op jit(solution)/shard_map/ppermute | solution.py:21
  463.4 7.9 collective-permute-start.76
  468.1 9.3 %collective-permute-start.85 = (f32[1,66,1]{2,1,0:T(8,128)S(1)}, f32[1,66,1]{2,1,0:T(8,128)S(1)}, u32[]{:S(2)}, u32[]{:S(2)}) collective-permute-start(f32[1,66,1]{2,1,0:T(8,128)S(1)} %get-tuple-element.160), channel_id=1, source_target_pairs={{0,1},{1,2},{2,3},{4,5},{5,6},{6,7},{8,9},{9,10},{10,11},{12,13},{... | collective-permute-start | bytes 800 | tf_op jit(solution)/shard_map/ppermute | solution.py:21
  (103 other events, 562.4 us)
where the time goes:
time: 846 us; the launch traced here: 833 us
  starting transfers between devices  329 us (39%)
  waiting for transfers between devices  258 us (30%)
  local copies, waits for them, and re-layouts  189 us (22%)
  other arithmetic  54.8 us (6%)
    ppermute x70, starting transfers between devices, with_halo(): lax.ppermute(head, axis, [((i + 1) % count, i) for i in range(ends)])  173 us
    ppermute x70, starting transfers between devices, with_halo(): lax.ppermute(tail, axis, [(i, (i + 1) % count) for i in range(ends)])  137 us
    ppermute x70, waiting for transfers between devices, with_halo(): lax.ppermute(head, axis, [((i + 1) % count, i) for i in range(ends)])  131 us
    ppermute x70, waiting for transfers between devices, with_halo(): lax.ppermute(tail, axis, [(i, (i + 1) % count) for i in range(ends)])  92.5 us
    unnamed x18, local copies, waits for them, and re-layouts  63.9 us
    reshape x4, local copies, waits for them, and re-layouts, restrict(): blocks = field_in.reshape(leading + (height // 2, 2, breadth // 2, 2))  56.2 us
    slice x3, local copies, waits for them, and re-layouts, restrict(): blocks[..., :, 0, :, 1]  50 us
    ppermute x10, waiting for transfers between devices, from_behind(): return lax.ppermute(block, axis, route)  34.3 us
  transfers between devices with their start and end apart: 150, of which 92 were waited for; matrix products, arithmetic and copies ran while one was open for 20% of the time, Pallas kernels for 0%

commit v1 on v0

v1 whole, which is shorter than its diff:
```python
import jax
import jax.numpy as jnp
from jax import lax
from jax.experimental import pallas as pl
from jax.experimental.pallas import tpu as pltpu
from jax.sharding import PartitionSpec as P

MESH = pl.DeviceIdType.MESH
FINE = 4
TIME_STEP = 0.035

ROWS, COLS, HALO = 128, 384, 16
EXT = ROWS + 2 * HALO
T_FINE = EXT // 8
T_COARSE = T_FINE // 2
CROWS = ROWS // 2
T_CHAIN = (CROWS + 32) // 8
LOW, HIGH = 16, 112
OWN, FROM_N, FROM_S, FROM_L, FROM_R, FROM_NL, FROM_NR, FROM_SL, FROM_SR = range(9)


def roll(x, shift, axis):
    shift = shift % x.shape[axis]
    return pltpu.roll(x, shift, axis) if shift else x


def flux_pass(src, coef, drift, T, W, emit):
    def load(t):
        values = [src[t, w] for w in range(W)]
        return values, [coef[t, w] * (2.0 + jnp.tanh(values[w])) for w in range(W)]

    def flux(v, k, vn, kn):
        return (k + kn) * (vn - v)

    first, last = load(0), load(T - 1)
    final = [flux(last[0][w], last[1][w], roll(first[0][w], -1, 0), roll(first[1][w], -1, 0)) for w in range(W)]
    above = [roll(f, 1, 0) for f in final]
    here = first
    for t in range(T):
        v, k = here
        if t < T - 1:
            following = last if t + 1 == T - 1 else load(t + 1)
            below = [flux(v[w], k[w], following[0][w], following[1][w]) for w in range(W)]
        else:
            following, below = None, final
        east = [flux(v[w], k[w], v[w + 1], k[w + 1]) for w in range(W - 1)]
        east.append(flux(v[W - 1], k[W - 1], roll(v[0], -1, 1), roll(k[0], -1, 1)))
        west = [roll(east[W - 1], 1, 1)] + east[:-1]
        for w in range(W):
            total = (v[w] + drift[t, w]) + ((east[w] - west[w]) + (below[w] - above[w]))
            emit(t, w, v[w], total)
        here, above = following, below


def heun(state, section, coef, drift, T, W, lanes, row_masks, emit=None):
    def keep(t, w, x):
        if w in (0, W - 1):
            x = x * lanes
        if t in row_masks:
            x = x * row_masks[t]
        return x

    def first(t, w, value, total):
        section[t, w] = keep(t, w, total)

    def second(t, w, value, total):
        result = keep(t, w, 0.5 * (state[t, w] + total))
        if emit is None:
            state[t, w] = result
        else:
            emit(t, w, result)

    flux_pass(state, coef, drift, T, W, first)
    flux_pass(section, coef, drift, T, W, second)


def pieces(x):
    top = x.astype(jnp.bfloat16)
    rest = x - top.astype(jnp.float32)
    middle = rest.astype(jnp.bfloat16)
    low = (rest - middle.astype(jnp.float32)).astype(jnp.bfloat16)
    return top, middle, low


def move_columns(x, choice):
    top, middle, low = [jnp.dot(part, choice, preferred_element_type=jnp.float32) for part in pieces(x)]
    return (top + middle) + low


def kernel(
    initial, guesses, conduct, source, out,
    X, Y, PS, PR, V, A, CH, SD, SPREAD, GATHER, RN, RX, RV, CA, CC, CSD, NAT, PK, E, PE, V12, A12, C12, S12, CN, CB, OUT,
    load_sem, store_sem, send1, recv1, send_relaxed, recv_relaxed, send3, recv3, send_coef, send_share, recv_share, ready,
):
    nt, nx, ny = lax.axis_size("tm"), lax.axis_size("sx"), lax.axis_size("sy")
    me, row, col = lax.axis_index("tm"), lax.axis_index("sx"), lax.axis_index("sy")
    chip, core = me // 2, lax.rem(me, 2)
    last = nt - 1
    north, south = lax.rem(row + nx - 1, nx), lax.rem(row + 1, nx)
    left, right = lax.rem(col + ny - 1, ny), lax.rem(col + 1, ny)
    spatial = [(north, col), (south, col), (row, left), (row, right),
               (north, left), (north, right), (south, left), (south, right)]

    barrier = pltpu.get_barrier_semaphore()
    for r, c in spatial:
        pl.semaphore_signal(barrier, inc=1, device_id=(me, r, c), device_id_type=MESH)
    for step in range(1, nt):
        pl.semaphore_signal(barrier, inc=1, device_id=(lax.rem(me + step, nt), row, col), device_id_type=MESH)

    def own_load(field, ref):
        return pltpu.make_async_copy(ref, X.at[field, HALO:HALO + ROWS, 0:COLS], load_sem.at[field])

    @pl.when(me == last)
    def _():
        own_load(0, initial).start()

    @pl.when(me != last)
    def _():
        own_load(0, guesses.at[0]).start()

    own_load(1, conduct).start()
    own_load(2, source).start()

    lane = lax.broadcasted_iota(jnp.int32, (8, 128), 1)
    sublane = lax.broadcasted_iota(jnp.int32, (8, 128), 0)
    one, zero = jnp.ones((8, 128), jnp.float32), jnp.zeros((8, 128), jnp.float32)
    at_top, at_bottom, at_left, at_right = row == 0, row == nx - 1, col == 0, col == ny - 1
    in_lanes = jnp.where(jnp.logical_or(jnp.logical_and(lane < LOW, at_left), jnp.logical_and(lane >= HIGH, at_right)), zero, one)

    def strip_mask(which, edge):
        return jnp.where(jnp.logical_and(sublane == which, edge), zero, one)

    n = lax.broadcasted_iota(jnp.int32, (512, 512), 0)
    o = lax.broadcasted_iota(jnp.int32, (512, 512), 1)
    place = (o & 127) * 4 + (o >> 7)
    from_n = jnp.where(n < COLS, n + 64, jnp.where(n < COLS + HALO, n + 64, jnp.where(n >= 512 - HALO, n - 448, -1)))
    SPREAD[...] = jnp.where(place == from_n, 1.0, 0.0).astype(jnp.bfloat16)
    n = lax.broadcasted_iota(jnp.int32, (512, COLS), 1)
    o = lax.broadcasted_iota(jnp.int32, (512, COLS), 0)
    GATHER[...] = jnp.where((o & 127) * 4 + (o >> 7) == n + 64, 1.0, 0.0).astype(jnp.bfloat16)

    pl.semaphore_wait(barrier, 8 + nt - 1)

    def row_copy(field, ref, side):
        where = (north, col) if side == 0 else (south, col)
        src = ref.at[0:HALO, :] if side == 0 else ref.at[ROWS - HALO:ROWS, :]
        dst = X.at[field, HALO + ROWS:EXT, 0:COLS] if side == 0 else X.at[field, 0:HALO, 0:COLS]
        k = field * 2 + side
        return pltpu.make_async_remote_copy(src, dst, send1.at[k], recv1.at[k], (me,) + where, MESH)

    @pl.when(me == last)
    def _():
        for side in range(2):
            row_copy(0, initial, side).start()

    @pl.when(me != last)
    def _():
        for side in range(2):
            row_copy(0, guesses.at[0], side).start()

    for field, ref in ((1, conduct), (2, source)):
        for side in range(2):
            row_copy(field, ref, side).start()

    group = lane // 16
    for field in range(3):
        own_load(field, conduct).wait()
        for side in range(2):
            for half in range(2):
                packed = None
                for q in range(8):
                    r0 = HALO + 64 * half + 8 * q
                    block = X[field, r0:r0 + 8, 0:128] if side == 0 else X[field, r0:r0 + 8, COLS - 128:COLS]
                    block = roll(block, 16 * q if side == 0 else 16 * q + 16, 1)
                    packed = block if packed is None else jnp.where(group == q, block, packed)
                PS[side, half, field] = packed

    def column_copies():
        plan = [
            (PS.at[1], PR.at[0:2], 6, (row, right)),
            (PS.at[0], PR.at[2:4], 7, (row, left)),
            (PS.at[1, 1], PR.at[4], 8, (south, right)),
            (PS.at[0, 1], PR.at[5], 9, (south, left)),
            (PS.at[1, 0], PR.at[6], 10, (north, right)),
            (PS.at[0, 0], PR.at[7], 11, (north, left)),
        ]
        return [pltpu.make_async_remote_copy(s, d, send1.at[k], recv1.at[k], (me,) + w, MESH) for s, d, k, w in plan]

    for copy in column_copies():
        copy.start()
    for copy in column_copies():
        copy.wait_recv()
    for field in range(3):
        for side in range(2):
            row_copy(field, conduct, side).wait_recv()

    for step in range(1, nt):
        pl.semaphore_signal(ready, inc=1, device_id=(lax.rem(me + step, nt), row, col), device_id_type=MESH)

    for field in range(3):
        for e in range(EXT // 8):
            if e < 2:
                from_left, from_right, q = PR[4, field], PR[5, field], 6 + e
            elif e >= 18:
                from_left, from_right, q = PR[6, field], PR[7, field], e - 18
            else:
                half, q = (e - 2) // 8, (e - 2) % 8
                from_left, from_right = PR[half, field], PR[2 + half, field]
            value = jnp.where(lane < 64, roll(from_right, -16 * q, 1), roll(from_left, 112 - 16 * q, 1))
            X[field, 8 * e:8 * e + 8, COLS:512] = value

    top16, bottom16 = strip_mask(0, at_top), strip_mask(7, at_bottom)

    def fine_mask(t):
        m = in_lanes
        if t < HALO:
            m = m * top16
        if t >= T_FINE - HALO:
            m = m * bottom16
        return m

    for field, dest, factor in ((0, V, 1.0), (1, CH, 0.25 * TIME_STEP), (2, SD, TIME_STEP)):
        spread = move_columns(X[field], SPREAD[...])
        for w in range(4):
            Y[w] = spread[:, 128 * w:128 * w + 128]
        for t in range(T_FINE):
            m = fine_mask(t) * factor
            for w in range(4):
                dest[t, w] = Y[w, pl.ds(t, 8, stride=T_FINE), :] * m

    def four(ref, t, w):
        return (ref[2 * t, 2 * w] + ref[2 * t, 2 * w + 1]) + (ref[2 * t + 1, 2 * w] + ref[2 * t + 1, 2 * w + 1])

    def pack_coarse(slot):
        eighth = lane // 8
        for side in range(2):
            packed = None
            for rb in range(8):
                for w in range(2):
                    q = rb * 2 + w
                    block = NAT[slot, w, 8 + 8 * rb:16 + 8 * rb, :]
                    block = roll(block, 8 * q - LOW if side == 0 else 8 * q - (HIGH - 8), 1)
                    packed = block if packed is None else jnp.where(eighth == q, block, packed)
            PK[slot, side] = packed

    def coarse_copies(source_slot, slot, tm, sems):
        nat, pk = NAT.at[source_slot], PK.at[source_slot]
        plan = [
            (nat.at[:, 8:8 + CROWS, :], E.at[slot, :, 16:16 + CROWS, :], OWN, (row, col)),
            (nat.at[:, CROWS - 8:CROWS + 8, :], E.at[slot, :, 0:16, :], FROM_N, (south, col)),
            (nat.at[:, 8:24, :], E.at[slot, :, 16 + CROWS:32 + CROWS, :], FROM_S, (north, col)),
            (pk.at[1], PE.at[slot, FROM_L], FROM_L, (row, right)),
            (pk.at[0], PE.at[slot, FROM_R], FROM_R, (row, left)),
            (pk.at[1], PE.at[slot, FROM_NL], FROM_NL, (south, right)),
            (pk.at[0], PE.at[slot, FROM_NR], FROM_NR, (south, left)),
            (pk.at[1], PE.at[slot, FROM_SL], FROM_SL, (north, right)),
            (pk.at[0], PE.at[slot, FROM_SR], FROM_SR, (north, left)),
        ]
        return [pltpu.make_async_remote_copy(s, d, sems.at[k], recv3.at[slot, k], (tm,) + w, MESH) for s, d, k, w in plan]

    for t in range(T_COARSE):
        for w in range(2):
            c, s = 0.25 * four(CH, t, w), four(SD, t, w)
            CC[t, w] = c
            CSD[t, w] = s
            NAT[1, w, pl.ds(t, 8, stride=T_COARSE), :] = c
            NAT[2, w, pl.ds(t, 8, stride=T_COARSE), :] = s
    for k in (1, 2):
        pack_coarse(k)
        for copy in coarse_copies(k, 6 + k, me, send_coef.at[k - 1])[1:]:
            copy.start()
        for w in range(2):
            E[6 + k, w, 16:16 + CROWS, :] = NAT[k, w, 8:8 + CROWS, :]

    fine_rows = {HALO - 1: top16, T_FINE - HALO: bottom16}

    def fine_run():
        def body(i, carry):
            heun(V, A, CH, SD, T_FINE, 4, in_lanes, fine_rows)
            return carry

        lax.fori_loop(0, FINE, body, 0)

    fine_run()

    for t in range(T_FINE):
        for w in range(4):
            RN[w, pl.ds(t, 8, stride=T_FINE), :] = V[t, w]
    relaxed_copy = pltpu.make_async_remote_copy(
        RN.at[:, HALO:HALO + ROWS, :], RX, send_relaxed, recv_relaxed, (lax.rem(me + 1, nt), row, col), MESH)
    relaxed_copy.start()
    for t in range(T_COARSE):
        for w in range(2):
            RV[t, w] = 0.25 * four(V, t, w)

    fine_run()

    share_of_psi = jnp.where(me == last, 0.0, 1.0)

    def target(t, w, result):
        NAT[0, w, pl.ds(t, 8, stride=T_COARSE), :] = 0.25 * four(V, t, w) - share_of_psi * result

    coarse_rows = {HALO // 2 - 1: top16, T_COARSE - HALO // 2: bottom16}
    heun(RV, CA, CC, CSD, T_COARSE, 2, in_lanes, coarse_rows, target)
    pack_coarse(0)
    pl.semaphore_wait(ready, nt - 1)

    slot_out = jnp.where(me == last, 0, me + 1)

    def each_receiver(action):
        for chip_to in range(nt // 2):
            wanted = jnp.logical_or(me == last, jnp.logical_and(chip_to > chip, me < last - 1))
            copies = coarse_copies(0, slot_out, 2 * chip_to + 1, send3.at[chip_to])

            @pl.when(wanted)
            def _():
                if chip_to == nt // 2 - 1:
                    @pl.when(me != last)
                    def _():
                        action(copies[0])
                else:
                    action(copies[0])
                for copy in copies[1:]:
                    action(copy)

    each_receiver(lambda copy: copy.start())

    def unpack(slot, store):
        for rb in range(12):
            if rb < 2:
                from_left, from_right, own = PE[slot, FROM_NL], PE[slot, FROM_NR], 6 + rb
            elif rb >= 10:
                from_left, from_right, own = PE[slot, FROM_SL], PE[slot, FROM_SR], rb - 10
            else:
                from_left, from_right, own = PE[slot, FROM_L], PE[slot, FROM_R], rb - 2
            for w in range(2):
                q = own * 2 + w
                value = E[slot, w, 8 * rb:8 * rb + 8, :]
                value = jnp.where(lane < LOW, roll(from_left, LOW - 8 - 8 * q, 1), value)
                value = jnp.where(lane >= HIGH, roll(from_right, HIGH - 8 * q, 1), value)
                mask = in_lanes
                if rb < 2:
                    mask = mask * jnp.where(at_top, 0.0, 1.0)
                if rb >= 10:
                    mask = mask * jnp.where(at_bottom, 0.0, 1.0)
                E[slot, w, 8 * rb:8 * rb + 8, :] = value * mask
        for t in range(T_CHAIN):
            for w in range(2):
                store(t, w, E[slot, w, pl.ds(t, 8, stride=T_CHAIN), :])

    def await_slot(slot, own=True):
        copies = coarse_copies(0, slot, me, send3.at[0])
        for copy in copies if own else copies[1:]:
            copy.wait_recv()

    chain_rows = {15 % T_CHAIN: strip_mask(15 // T_CHAIN, at_top), 80 % T_CHAIN: strip_mask(80 // T_CHAIN, at_bottom)}

    for slot in (7, 8):
        await_slot(slot, own=False)

    share = pltpu.make_async_remote_copy(
        CB.at[:, 16:16 + CROWS, :], CN.at[:, 16:16 + CROWS, :], send_share, recv_share, (jnp.maximum(me - 1, 0), row, col), MESH)

    @pl.when(core == 1)
    def _():
        def put(ref):
            def store(t, w, x):
                ref[t, w] = x
            return store

        unpack(7, put(C12))
        unpack(8, put(S12))

        @pl.when(me == last)
        def _():
            for w in range(2):
                E[0, w, 16:16 + CROWS, :] = NAT[0, w, 8:8 + CROWS, :]

        @pl.when(me != last)
        def _():
            coarse_copies(0, 0, me, send3.at[0])[0].wait_recv()

        await_slot(0, own=False)
        unpack(0, put(V12))

        def advance(slot):
            await_slot(slot)
            heun(V12, A12, C12, S12, T_CHAIN, 2, in_lanes, chain_rows)

            def add(t, w, x):
                V12[t, w] = V12[t, w] + x

            unpack(slot, add)

        def natural(ref):
            for t in range(T_CHAIN):
                for w in range(2):
                    ref[w, pl.ds(t, 8, stride=T_CHAIN), :] = V12[t, w]

        def body(slot, carry):
            @pl.when(slot == me - 1)
            def _():
                natural(CB)
                share.start()

            advance(slot)
            return carry

        lax.fori_loop(1, me, body, 0)
        natural(CN)

        @pl.when(me > 1)
        def _():
            share.wait_send()

    relaxed_copy.wait_recv()

    def relaxed_four(t, w):
        def at(tt, ww):
            return RX[ww, pl.ds(tt, 8, stride=16), :]
        return 0.25 * ((at(2 * t, 2 * w) + at(2 * t, 2 * w + 1)) + (at(2 * t + 1, 2 * w) + at(2 * t + 1, 2 * w + 1)))

    @pl.when(jnp.logical_and(core == 0, me > 0))
    def _():
        share.wait_recv()

    @pl.when(me == 0)
    def _():
        for t in range(8):
            for w in range(2):
                CN[w, pl.ds(16 + t, 8, stride=8), :] = relaxed_four(t, w)

    for t in range(8):
        for w in range(2):
            change = CN[w, pl.ds(16 + t, 8, stride=8), :] - relaxed_four(t, w)
            for tt in (2 * t, 2 * t + 1):
                for ww in (2 * w, 2 * w + 1):
                    Y[ww, pl.ds(tt, 8, stride=16), :] = RX[ww, pl.ds(tt, 8, stride=16), :] + change

    corrected = jnp.concatenate([Y[w, 0:ROWS, :] for w in range(4)], axis=1)
    OUT[...] = move_columns(corrected, GATHER[...])
    store = pltpu.make_async_copy(OUT, out.at[0], store_sem)
    store.start()

    for field in range(3):
        for side in range(2):
            row_copy(field, conduct, side).wait_send()
    for copy in column_copies():
        copy.wait_send()
    for k in (1, 2):
        for copy in coarse_copies(k, 6 + k, me, send_coef.at[k - 1])[1:]:
            copy.wait_send()
    relaxed_copy.wait_send()
    each_receiver(lambda copy: copy.wait_send())
    store.wait()


def local(initial, guesses, conduct, source):
    nt = lax.axis_size("tm")
    f32, bf16 = jnp.float32, jnp.bfloat16
    vmem, dma = pltpu.VMEM, pltpu.SemaphoreType.DMA
    fine, coarse, chain = (T_FINE, 4, 8, 128), (T_COARSE, 2, 8, 128), (T_CHAIN, 2, 8, 128)
    scratch = [
        vmem((3, EXT, 512), f32),
        vmem((4, EXT, 128), f32),
        vmem((2, 2, 3, 8, 128), f32),
        vmem((8, 3, 8, 128), f32),
        vmem(fine, f32),
        vmem(fine, f32),
        vmem(fine, f32),
        vmem(fine, f32),
        vmem((512, 512), bf16),
        vmem((512, COLS), bf16),
        vmem((4, EXT, 128), f32),
        vmem((4, ROWS, 128), f32),
        vmem(coarse, f32),
        vmem(coarse, f32),
        vmem(coarse, f32),
        vmem(coarse, f32),
        vmem((3, 2, EXT // 2, 128), f32),
        vmem((3, 2, 8, 128), f32),
        vmem((9, 2, CROWS + 32, 128), f32),
        vmem((9, 9, 8, 128), f32),
        vmem(chain, f32),
        vmem(chain, f32),
        vmem(chain, f32),
        vmem(chain, f32),
        vmem((2, CROWS + 32, 128), f32),
        vmem((2, CROWS + 32, 128), f32),
        vmem((ROWS, COLS), f32),
        dma((3,)), dma, dma((12,)), dma((12,)), dma, dma, dma((nt // 2, 9)), dma((9, 9)), dma((2, 9)), dma, dma,
        pltpu.SemaphoreType.REGULAR,
    ]
    return pl.pallas_call(
        kernel,
        out_shape=jax.ShapeDtypeStruct(guesses.shape, f32),
        in_specs=[pl.BlockSpec(memory_space=pl.ANY)] * 4,
        out_specs=pl.BlockSpec(memory_space=pl.ANY),
        scratch_shapes=scratch,
        compiler_params=pltpu.CompilerParams(collective_id=0, has_side_effects=True, vmem_limit_bytes=32 * 1024 * 1024),
    )(initial, guesses, conduct, source)


def solution(mesh):
    in_specs = (P("sx", "sy"), P("tm", "sx", "sy"), P("sx", "sy"), P("sx", "sy"))
    out_specs = P("tm", "sx", "sy")
    return jax.shard_map(local, mesh=mesh, in_specs=in_specs, out_specs=out_specs, check_vma=False)
```

time: 846 us -> 31.8 us (0.04)
  the two profiles are of different devices: /device:TPU:112 before, /device:TPU:25 now
where the time goes in v1:
time: 31.8 us; the launch traced here: 31.5 us
  Pallas kernels  27.1 us (85%)
  local copies, waits for them, and re-layouts  4.38 us (14%)
    pallas_call x1, Pallas kernels, local(): pl.pallas_call(kernel, out_shape=jax.ShapeDtypeStruct(guesses.shape, f32)...  27.1 us
    unnamed x9, local copies, waits for them, and re-layouts  4.38 us

profile of v1, /device:TPU:25, one launch (start us, length us, event | category | flops | bytes accessed | tf_op | source)
XLA Modules:
  0.0 31.5 jit_solution(13635606040049467124)
XLA Ops:
  0.0 0.0 copy-start
  0.0 0.9 %copy-done = f32[128,384]{1,0:T(8,128)S(1)} copy-done((f32[128,384]{1,0:T(8,128)S(1)}, f32[128,384]{1,0:T(8,128)}, u32[]{:S(2)}) %copy-start) | copy-done | bytes 196632
  0.9 0.0 copy-start.1
  0.9 0.9 %copy-done.1 = f32[1,128,384]{2,1,0:T(8,128)S(1)} copy-done((f32[1,128,384]{2,1,0:T(8,128)S(1)}, f32[1,128,384]{2,1,0:T(8,128)}, u32[]{:S(2)}) %copy-start.1) | copy-done | bytes 196632
  1.9 0.0 copy-start.2
  1.9 0.9 %copy-done.2 = f32[128,384]{1,0:T(8,128)S(1)} copy-done((f32[128,384]{1,0:T(8,128)S(1)}, f32[128,384]{1,0:T(8,128)}, u32[]{:S(2)}) %copy-start.2) | copy-done | bytes 196632
  2.8 0.0 copy-start.3
  2.8 0.9 %copy-done.3 = f32[128,384]{1,0:T(8,128)S(1)} copy-done((f32[128,384]{1,0:T(8,128)S(1)}, f32[128,384]{1,0:T(8,128)}, u32[]{:S(2)}) %copy-start.3) | copy-done | bytes 196632
  3.7 27.1 %shard_map.46 = f32[1,128,384]{2,1,0:T(8,128)S(1)} custom-call(f32[128,384]{1,0:T(8,128)S(1)} %copy-done, f32[1,128,384]{2,1,0:T(8,128)S(1)} %copy-done.1, f32[128,384]{1,0:T(8,128)S(1)} %copy-done.2, f32[128,384]{1,0:T(8,128)S(1)} %copy-done.3), custom_call_target="tpu_custom_call" | custom-call | tf_op jit(solution)/shard_map/pallas_call | solution.py:494
  30.9 0.7 %copy.6 = f32[1,128,384]{2,1,0:T(8,128)} copy(f32[1,128,384]{2,1,0:T(8,128)S(1)} %shard_map.46) | data formatting | bytes 393216
Async XLA Ops:
  0.0 0.9 %copy-start = (f32[128,384]{1,0:T(8,128)S(1)}, f32[128,384]{1,0:T(8,128)}, u32[]{:S(2)}) copy-start(f32[128,384]{1,0:T(8,128)} %initial.1) | copy-start | bytes 589828
  0.9 0.9 %copy-start.1 = (f32[1,128,384]{2,1,0:T(8,128)S(1)}, f32[1,128,384]{2,1,0:T(8,128)}, u32[]{:S(2)}) copy-start(f32[1,128,384]{2,1,0:T(8,128)} %guesses.1) | copy-start | bytes 589828
  1.9 0.9 %copy-start.2 = (f32[128,384]{1,0:T(8,128)S(1)}, f32[128,384]{1,0:T(8,128)}, u32[]{:S(2)}) copy-start(f32[128,384]{1,0:T(8,128)} %conduct.1) | copy-start | bytes 589828
  2.8 0.9 %copy-start.3 = (f32[128,384]{1,0:T(8,128)S(1)}, f32[128,384]{1,0:T(8,128)}, u32[]{:S(2)}) copy-start(f32[128,384]{1,0:T(8,128)} %source.1) | copy-start | bytes 589828

commit v2 on v1

v2 whole, which is shorter than its diff:
```python
import jax
import jax.numpy as jnp
from jax import lax
from jax.experimental import pallas as pl
from jax.experimental.pallas import tpu as pltpu
from jax.sharding import PartitionSpec as P

MESH = pl.DeviceIdType.MESH
FINE = 4
TIME_STEP = 0.035

ROWS, COLS, HALO = 128, 384, 16
EXT = ROWS + 2 * HALO
T_FINE = EXT // 8
T_COARSE = T_FINE // 2
CROWS = ROWS // 2
T_CHAIN = (CROWS + 32) // 8
LOW, HIGH = 16, 112
OWN, FROM_N, FROM_S, FROM_L, FROM_R, FROM_NL, FROM_NR, FROM_SL, FROM_SR, SLOT = 0, 12, 15, 18, 19, 20, 21, 22, 23, 24
R_N, R_S, R_L, R_R, R_NL, R_NR, R_SL, R_SR, R_ALL = 0, 18, 36, 48, 60, 63, 66, 69, 72


def roll(x, shift, axis):
    shift = shift % x.shape[axis]
    return pltpu.roll(x, shift, axis) if shift else x


def flux_pass(src, coef, drift, T, W, emit):
    def load(t):
        values = [src[t, w] for w in range(W)]
        return values, [coef[t, w] * (2.0 + jnp.tanh(values[w])) for w in range(W)]

    def flux(v, k, vn, kn):
        return (k + kn) * (vn - v)

    first, last = load(0), load(T - 1)
    final = [flux(last[0][w], last[1][w], roll(first[0][w], -1, 0), roll(first[1][w], -1, 0)) for w in range(W)]
    above = [roll(f, 1, 0) for f in final]
    here = first
    for t in range(T):
        v, k = here
        if t < T - 1:
            following = last if t + 1 == T - 1 else load(t + 1)
            below = [flux(v[w], k[w], following[0][w], following[1][w]) for w in range(W)]
        else:
            following, below = None, final
        east = [flux(v[w], k[w], v[w + 1], k[w + 1]) for w in range(W - 1)]
        east.append(flux(v[W - 1], k[W - 1], roll(v[0], -1, 1), roll(k[0], -1, 1)))
        west = [roll(east[W - 1], 1, 1)] + east[:-1]
        for w in range(W):
            total = (v[w] + drift[t, w]) + ((east[w] - west[w]) + (below[w] - above[w]))
            emit(t, w, v[w], total)
        here, above = following, below


def heun(state, section, coef, drift, T, W, lanes, row_masks, emit=None):
    def keep(t, w, x):
        if w in (0, W - 1):
            x = x * lanes
        if t in row_masks:
            x = x * row_masks[t]
        return x

    def first(t, w, value, total):
        section[t, w] = keep(t, w, total)

    def second(t, w, value, total):
        result = keep(t, w, 0.5 * (state[t, w] + total))
        if emit is None:
            state[t, w] = result
        else:
            emit(t, w, result)

    flux_pass(state, coef, drift, T, W, first)
    flux_pass(section, coef, drift, T, W, second)


def pieces(x):
    top = x.astype(jnp.bfloat16)
    rest = x - top.astype(jnp.float32)
    middle = rest.astype(jnp.bfloat16)
    low = (rest - middle.astype(jnp.float32)).astype(jnp.bfloat16)
    return top, middle, low


def move_columns(x, choice):
    top, middle, low = [jnp.dot(part, choice, preferred_element_type=jnp.float32) for part in pieces(x)]
    return (top + middle) + low


def pack_group(x, own):
    return [jnp.where(own, x[k], roll(x[3], 96 - 32 * k, 1)) for k in range(3)]


def unpack_group(y, lane):
    parts = [roll(y[k], 32 * k - 96, 1) for k in range(3)]
    return list(y) + [jnp.where(lane < LOW + 32, parts[0], jnp.where(lane < LOW + 64, parts[1], parts[2]))]


def kernel(
    initial, guesses, conduct, source, out,
    X, Y, SR, SC, R1, V, A, CH, SD, SPREAD, GATHER, PROLONG, RN, RS, RX, RR, BASE, RV, CA, CC, CSD, NAT, SB, EB, NB,
    V12, A12, C12, S12, CN, CB, OUT,
    load_sem, store_sem, send1, recv1, send_relaxed, recv_relaxed, send3, recv3, send_coef, send_share, recv_share, ready,
):
    nt, nx, ny = lax.axis_size("tm"), lax.axis_size("sx"), lax.axis_size("sy")
    me, row, col = lax.axis_index("tm"), lax.axis_index("sx"), lax.axis_index("sy")
    chip, core = me // 2, lax.rem(me, 2)
    chips, last = nt // 2, nt - 1
    north, south = lax.rem(row + nx - 1, nx), lax.rem(row + 1, nx)
    left, right = lax.rem(col + ny - 1, ny), lax.rem(col + 1, ny)
    spatial = [(north, col), (south, col), (row, left), (row, right),
               (north, left), (north, right), (south, left), (south, right)]

    barrier = pltpu.get_barrier_semaphore()
    for r, c in spatial:
        pl.semaphore_signal(barrier, inc=1, device_id=(me, r, c), device_id_type=MESH)
    for step in range(1, nt):
        pl.semaphore_signal(barrier, inc=1, device_id=(lax.rem(me + step, nt), row, col), device_id_type=MESH)

    @pl.when(me == last)
    def _():
        pltpu.make_async_copy(initial, X.at[0], load_sem).start()

    @pl.when(me != last)
    def _():
        pltpu.make_async_copy(guesses.at[0], X.at[0], load_sem).start()

    pltpu.make_async_copy(conduct, X.at[1], load_sem).start()
    pltpu.make_async_copy(source, X.at[2], load_sem).start()

    lane = lax.broadcasted_iota(jnp.int32, (8, 128), 1)
    sublane = lax.broadcasted_iota(jnp.int32, (8, 128), 0)
    one, zero = jnp.ones((8, 128), jnp.float32), jnp.zeros((8, 128), jnp.float32)
    own_lanes = jnp.logical_and(lane >= LOW, lane < HIGH)
    at_top, at_bottom, at_left, at_right = row == 0, row == nx - 1, col == 0, col == ny - 1
    in_lanes = jnp.where(jnp.logical_or(jnp.logical_and(lane < LOW, at_left), jnp.logical_and(lane >= HIGH, at_right)), zero, one)

    def strip_mask(which, edge):
        return jnp.where(jnp.logical_and(sublane == which, edge), zero, one)

    def fill(ref, rows, columns):
        ref[...] = jnp.where(rows == columns, 1.0, 0.0).astype(jnp.bfloat16)

    o = lax.broadcasted_iota(jnp.int32, (1, 512), 1)
    fill(SPREAD, lax.broadcasted_iota(jnp.int32, (COLS, 1), 0) + 64, (o & 127) * 4 + (o >> 7))
    o = lax.broadcasted_iota(jnp.int32, (COLS, 1), 0)
    k, l = o >> 7, o & 127
    inside = jnp.logical_and(l >= LOW, l < HIGH)
    packed_from = jnp.where(inside, 4 * l + k, 4 * (((l + 16) & 127) + LOW + 32 * k) + 3)
    fill(GATHER, packed_from, lax.broadcasted_iota(jnp.int32, (1, COLS), 1) + 64)
    o = lax.broadcasted_iota(jnp.int32, (256, 1), 0)
    fill(PROLONG, (o & 127) * 2 + (o >> 7), (lax.broadcasted_iota(jnp.int32, (1, COLS), 1) + 64) >> 1)

    pltpu.make_async_copy(X, X, load_sem).wait()

    for field, factor in ((0, None), (1, 0.25 * TIME_STEP), (2, TIME_STEP)):
        spread = move_columns(X[field], SPREAD[...])
        for w in range(4):
            part = spread[:, 128 * w:128 * w + 128]
            Y[field, w, HALO:HALO + ROWS, :] = part if factor is None else part * factor

    def own_block(field, w, rb):
        return Y[field, w, HALO + 8 * rb:HALO + 8 * rb + 8, :]

    for field in range(3):
        for side in range(2):
            for b in range(2):
                packed = pack_group([own_block(field, w, b if side == 0 else 14 + b) for w in range(4)], own_lanes)
                for k in range(3):
                    SR[side, field * 6 + b * 3 + k] = packed[k]
    eighth = lane // 8
    for field in range(3):
        for side in range(2):
            for quarter in range(4):
                packed = None
                for q in range(16):
                    block = own_block(field, q % 4, 4 * quarter + q // 4)
                    block = roll(block, 8 * q + 100 - LOW if side == 0 else 8 * q - (HIGH - 4), 1)
                    slot_of = (q + 12) % 16 if side == 0 else q
                    packed = block if packed is None else jnp.where(eighth == slot_of, block, packed)
                SC[side, quarter, field] = packed

    pl.semaphore_wait(barrier, 8 + nt - 1)

    first_exchange = [
        pltpu.make_async_remote_copy(s, R1.at[k:k + size], send1, recv1, (me,) + w, MESH)
        for s, k, size, w in [
            (SC.at[1, 3], R_NL, 3, (south, right)),
            (SC.at[0, 3], R_NR, 3, (south, left)),
            (SC.at[1, 0], R_SL, 3, (north, right)),
            (SC.at[0, 0], R_SR, 3, (north, left)),
            (SR.at[0], R_S, 18, (north, col)),
            (SR.at[1], R_N, 18, (south, col)),
        ]
    ]
    for side, k, w in ((1, R_L, (row, right)), (0, R_R, (row, left))):
        for quarter in range(4):
            first_exchange.append(pltpu.make_async_remote_copy(
                SC.at[side, quarter], R1.at[k + 3 * quarter:k + 3 * quarter + 3], send1, recv1, (me,) + w, MESH))
    for copy in first_exchange:
        copy.start()
    pltpu.make_async_copy(R1, R1, recv1).wait()

    for step in range(1, nt):
        pl.semaphore_signal(ready, inc=1, device_id=(lax.rem(me + step, nt), row, col), device_id_type=MESH)

    top16, bottom16 = strip_mask(0, at_top), strip_mask(7, at_bottom)
    masks = [in_lanes * (top16 if t < HALO else 1.0) * (bottom16 if t >= T_FINE - HALO else 1.0) for t in range(T_FINE)]
    odd_slot = (lane & 4) != 0
    for field, dest in ((1, CH), (0, V), (2, SD)):
        halo = {}
        for e in range(EXT // 8):
            if e < 2:
                l, r, rb = R_NL, R_NR, 14 + e
            elif e >= 18:
                l, r, rb = R_SL, R_SR, e - 18
            else:
                rb = e - 2
                l, r = R_L + 3 * (rb // 4), R_R + 3 * (rb // 4)
            if (l, r) not in halo:
                halo[l, r] = jnp.where(odd_slot, R1[r + field], R1[l + field])
            if e < 2 or e >= 18:
                start = (R_N + e * 3 if e < 2 else R_S + (e - 18) * 3) + field * 6
                values = unpack_group([R1[start + k] for k in range(3)], lane)
            else:
                values = [own_block(field, w, rb) for w in range(4)]
            for w in range(4):
                q = (rb % 4) * 4 + w
                Y[field, w, 8 * e:8 * e + 8, :] = jnp.where(own_lanes, values[w], roll(halo[l, r], LOW - 4 - 8 * q, 1))
        for t in range(T_FINE):
            for w in range(4):
                dest[t, w] = Y[field, w, pl.ds(t, 8, stride=T_FINE), :] * masks[t]

    def four(ref, t, w):
        return (ref[2 * t, 2 * w] + ref[2 * t, 2 * w + 1]) + (ref[2 * t + 1, 2 * w] + ref[2 * t + 1, 2 * w + 1])

    def pack_coarse(which):
        def block(rb, w):
            return NAT[which, w, 8 + 8 * rb:16 + 8 * rb, :]

        for g in range(4):
            packed = pack_group([block(2 * g + i // 2, i % 2) for i in range(4)], own_lanes)
            for k in range(3):
                SB[which, 3 * g + k] = packed[k]
        for side in range(2):
            packed = None
            for q in range(16):
                moved = roll(block(q // 2, q % 2), 8 * q - LOW if side == 0 else 8 * q - (HIGH - 8), 1)
                packed = moved if packed is None else jnp.where(eighth == q, moved, packed)
            SB[which, 12 + side] = packed

    def coarse_copies(which, slot, tm, send, recv):
        src = SB.at[which]
        plan = [
            (12, 1, FROM_SR, (north, left)),
            (13, 1, FROM_SL, (north, right)),
            (12, 1, FROM_NR, (south, left)),
            (13, 1, FROM_NL, (south, right)),
            (0, 3, FROM_S, (north, col)),
            (9, 3, FROM_N, (south, col)),
            (12, 1, FROM_R, (row, left)),
            (13, 1, FROM_L, (row, right)),
            (0, 12, OWN, (row, col)),
        ]
        return [pltpu.make_async_remote_copy(src.at[a:a + size], EB.at[slot, k:k + size], send, recv, (tm,) + w, MESH)
                for a, size, k, w in plan]

    for t in range(T_COARSE):
        for w in range(2):
            c, s = 0.25 * four(CH, t, w), four(SD, t, w)
            CC[t, w] = c
            CSD[t, w] = s
            NAT[1, w, pl.ds(t, 8, stride=T_COARSE), :] = c
            NAT[2, w, pl.ds(t, 8, stride=T_COARSE), :] = s

    coef_copies = [copy for k in (1, 2) for copy in coarse_copies(k, 6 + k, me, send_coef, recv3.at[7])[:8]]

    @pl.when(core == 1)
    def _():
        for k in (1, 2):
            pack_coarse(k)
        for copy in coef_copies:
            copy.start()
        for k in (1, 2):
            for v in range(12):
                EB[6 + k, v] = SB[k, v]

    fine_rows = {HALO - 1: top16, T_FINE - HALO: bottom16}

    def fine_run():
        def body(i, carry):
            heun(V, A, CH, SD, T_FINE, 4, in_lanes, fine_rows)
            return carry

        lax.fori_loop(0, FINE, body, 0)

    fine_run()

    for t in range(T_FINE):
        for w in range(4):
            RN[w, pl.ds(t, 8, stride=T_FINE), :] = V[t, w]
    for rb in range(16):
        packed = pack_group([RN[w, HALO + 8 * rb:HALO + 8 * rb + 8, :] for w in range(4)], own_lanes)
        for k in range(3):
            RS[k, 8 * rb:8 * rb + 8, :] = packed[k]
    relaxed_copy = pltpu.make_async_remote_copy(
        RS, RX, send_relaxed, recv_relaxed, (lax.rem(me + 1, nt), row, col), MESH)
    relaxed_copy.start()
    for t in range(T_COARSE):
        for w in range(2):
            RV[t, w] = 0.25 * four(V, t, w)

    fine_run()

    share_of_psi = jnp.where(me == last, 0.0, 1.0)

    def target(t, w, result):
        NAT[0, w, pl.ds(t, 8, stride=T_COARSE), :] = 0.25 * four(V, t, w) - share_of_psi * result

    coarse_rows = {HALO // 2 - 1: top16, T_COARSE - HALO // 2: bottom16}
    heun(RV, CA, CC, CSD, T_COARSE, 2, in_lanes, coarse_rows, target)
    pack_coarse(0)
    pl.semaphore_wait(ready, nt - 1)

    slot_out = jnp.where(me == last, 0, me + 1)
    is_last = me == last

    def each_receiver(action):
        for k in (2, 3, 1, 0):
            copies = coarse_copies(0, slot_out, 2 * lax.rem(chip + k, chips) + 1, send3.at[k], recv3.at[slot_out])
            if k == 0:
                @pl.when(is_last)
                def _():
                    action(k, copies[:8])
                continue
            reached = jnp.logical_or(is_last, jnp.logical_and(chip + k < chips, me < last - 1))
            tile_only = k == 1

            @pl.when(reached)
            def _():
                if tile_only:
                    @pl.when(core == 0)
                    def _():
                        action(k, copies)

                    @pl.when(core == 1)
                    def _():
                        action(k, copies[8:])
                else:
                    action(k, copies)

    def start(k, copies):
        for copy in copies:
            copy.start()

    def finish(k, copies):
        size = {8: 12, 9: 24, 1: 12}[len(copies)]
        whole = EB.at[0, 0:size]
        pltpu.make_async_copy(whole, whole, send3.at[k]).wait()

    each_receiver(start)

    def unpack(slot, store):
        def halo_at(e):
            if e < 2:
                return EB[slot, FROM_NL], EB[slot, FROM_NR], 6 + e
            if e >= 10:
                return EB[slot, FROM_SL], EB[slot, FROM_SR], e - 10
            return EB[slot, FROM_L], EB[slot, FROM_R], e - 2

        for g in range(6):
            base = FROM_N if g == 0 else FROM_S if g == 5 else OWN + 3 * (g - 1)
            values = unpack_group([EB[slot, base + k] for k in range(3)], lane)
            mask = in_lanes
            if g == 0:
                mask = mask * jnp.where(at_top, 0.0, 1.0)
            if g == 5:
                mask = mask * jnp.where(at_bottom, 0.0, 1.0)
            for i in range(4):
                e, w = 2 * g + i // 2, i % 2
                from_left, from_right, rb = halo_at(e)
                q = rb * 2 + w
                value = jnp.where(lane < LOW, roll(from_left, LOW - 8 - 8 * q, 1), values[i])
                value = jnp.where(lane >= HIGH, roll(from_right, HIGH - 8 * q, 1), value)
                NB[w, 8 * e:8 * e + 8, :] = value * mask
        for t in range(T_CHAIN):
            for w in range(2):
                store(t, w, NB[w, pl.ds(t, 8, stride=T_CHAIN), :])

    def await_vectors(ref, sem):
        pltpu.make_async_copy(ref, ref, sem).wait()

    chain_rows = {15 % T_CHAIN: strip_mask(15 // T_CHAIN, at_top), 80 % T_CHAIN: strip_mask(80 // T_CHAIN, at_bottom)}
    share = pltpu.make_async_remote_copy(
        CB, CN, send_share, recv_share, (jnp.maximum(me - 1, 0), row, col), MESH)

    def natural(ref):
        for t in range(T_CHAIN):
            for w in range(2):
                NB[w, pl.ds(t, 8, stride=T_CHAIN), :] = V12[t, w]
        for w in range(2):
            ref[w] = NB[w, 16:16 + CROWS, :]

    def relaxed_base():
        await_vectors(RX, recv_relaxed)
        for rb in range(16):
            values = unpack_group([RX[k, 8 * rb:8 * rb + 8, :] for k in range(3)], lane)
            for w in range(4):
                RN[w, 8 * rb:8 * rb + 8, :] = values[w]
        for t in range(8):
            for w in range(2):
                def at(tt, ww):
                    return RN[ww, pl.ds(tt, 8, stride=16), :]
                RR[t, w] = 0.25 * ((at(2 * t, 2 * w) + at(2 * t, 2 * w + 1)) + (at(2 * t + 1, 2 * w) + at(2 * t + 1, 2 * w + 1)))
        base = move_columns(jnp.concatenate([RX[k] for k in range(3)], axis=1), GATHER[...])
        for k in range(3):
            BASE[k] = base[:, 128 * k:128 * k + 128]

    @pl.when(core == 1)
    def _():
        def put(ref):
            def store(t, w, x):
                ref[t, w] = x
            return store

        await_vectors(EB.at[7:9, FROM_N:SLOT], recv3.at[7])
        unpack(7, put(C12))
        unpack(8, put(S12))

    relaxed_base()

    @pl.when(core == 1)
    def _():
        def put(t, w, x):
            V12[t, w] = x

        def add(t, w, x):
            V12[t, w] = V12[t, w] + x

        @pl.when(is_last)
        def _():
            for v in range(12):
                EB[0, v] = SB[0, v]
            await_vectors(EB.at[0, FROM_N:SLOT], recv3.at[0])

        @pl.when(me == 1)
        def _():
            await_vectors(EB.at[0, 0:FROM_N], recv3.at[0])

        @pl.when(jnp.logical_and(me != last, me > 1))
        def _():
            await_vectors(EB.at[0], recv3.at[0])

        unpack(0, put)

        def body(slot, carry):
            final = slot == me - 1

            @pl.when(final)
            def _():
                natural(CB)
                share.start()
                await_vectors(EB.at[slot, 0:FROM_N], recv3.at[slot])

            @pl.when(jnp.logical_not(final))
            def _():
                await_vectors(EB.at[slot], recv3.at[slot])

            heun(V12, A12, C12, S12, T_CHAIN, 2, in_lanes, chain_rows)
            unpack(slot, add)
            return carry

        lax.fori_loop(1, me, body, 0)
        natural(CN)

        @pl.when(me > 1)
        def _():
            share.wait_send()

    @pl.when(jnp.logical_and(core == 0, me > 0))
    def _():
        share.wait_recv()

    @pl.when(me == 0)
    def _():
        for t in range(8):
            for w in range(2):
                CN[w, pl.ds(t, 8, stride=8), :] = RR[t, w]

    change = jnp.concatenate(
        [jnp.concatenate([jnp.where(own_lanes, CN[w, pl.ds(t, 8, stride=8), :] - RR[t, w], 0.0) for w in range(2)], axis=1)
         for t in range(8)], axis=0)
    change = move_columns(change, PROLONG[...])
    for t in range(8):
        for k in range(3):
            for tt in (2 * t, 2 * t + 1):
                OUT[k, pl.ds(tt, 8, stride=16), :] = (
                    BASE[k, pl.ds(tt, 8, stride=16), :] + change[8 * t:8 * t + 8, 128 * k:128 * k + 128])
    for k in range(3):
        pltpu.make_async_copy(OUT.at[k], out.at[0, :, 128 * k:128 * k + 128], store_sem).start()

    await_vectors(R1, send1)

    @pl.when(core == 1)
    def _():
        await_vectors(EB.at[7:9, FROM_N:SLOT], send_coef)

    relaxed_copy.wait_send()
    each_receiver(finish)
    await_vectors(OUT, store_sem)


def local(initial, guesses, conduct, source):
    nt = lax.axis_size("tm")
    f32, bf16 = jnp.float32, jnp.bfloat16
    vmem, dma = pltpu.VMEM, pltpu.SemaphoreType.DMA
    fine, coarse, chain = (T_FINE, 4, 8, 128), (T_COARSE, 2, 8, 128), (T_CHAIN, 2, 8, 128)
    scratch = [
        vmem((3, ROWS, COLS), f32),
        vmem((3, 4, EXT, 128), f32),
        vmem((2, 18, 8, 128), f32),
        vmem((2, 4, 3, 8, 128), f32),
        vmem((R_ALL, 8, 128), f32),
        vmem(fine, f32),
        vmem(fine, f32),
        vmem(fine, f32),
        vmem(fine, f32),
        vmem((COLS, 512), bf16),
        vmem((COLS, COLS), bf16),
        vmem((256, COLS), bf16),
        vmem((4, EXT, 128), f32),
        vmem((3, ROWS, 128), f32),
        vmem((3, ROWS, 128), f32),
        vmem((8, 2, 8, 128), f32),
        vmem((3, ROWS, 128), f32),
        vmem(coarse, f32),
        vmem(coarse, f32),
        vmem(coarse, f32),
        vmem(coarse, f32),
        vmem((3, 2, EXT // 2, 128), f32),
        vmem((3, 14, 8, 128), f32),
        vmem((9, SLOT, 8, 128), f32),
        vmem((2, CROWS + 32, 128), f32),
        vmem(chain, f32),
        vmem(chain, f32),
        vmem(chain, f32),
        vmem(chain, f32),
        vmem((2, CROWS, 128), f32),
        vmem((2, CROWS, 128), f32),
        vmem((3, ROWS, 128), f32),
        dma, dma, dma, dma, dma, dma, dma((nt // 2,)), dma((8,)), dma, dma, dma,
        pltpu.SemaphoreType.REGULAR,
    ]
    return pl.pallas_call(
        kernel,
        out_shape=jax.ShapeDtypeStruct(guesses.shape, f32),
        in_specs=[pl.BlockSpec(memory_space=pl.ANY)] * 4,
        out_specs=pl.BlockSpec(memory_space=pl.ANY),
        scratch_shapes=scratch,
        compiler_params=pltpu.CompilerParams(collective_id=0, has_side_effects=True, vmem_limit_bytes=60 * 1024 * 1024),
    )(initial, guesses, conduct, source)


def solution(mesh):
    in_specs = (P("sx", "sy"), P("tm", "sx", "sy"), P("sx", "sy"), P("sx", "sy"))
    out_specs = P("tm", "sx", "sy")
    return jax.shard_map(local, mesh=mesh, in_specs=in_specs, out_specs=out_specs, check_vma=False)
```

time: 31.8 us -> 25.7 us (0.81)
  Pallas kernels: 27.1 us -> 23.9 us
  local copies, waits for them, and re-layouts: 4.38 us -> 1.62 us
    pallas_call x1, Pallas kernels: 27.1 us -> 23.9 us  [local(): pl.pallas_call(kernel, out_shape=jax.ShapeDtypeStruct(guesses.shape, f32)...]
    unnamed x9 -> x1, local copies, waits for them, and re-layouts: 4.38 us -> 1.62 us
where the time goes in v2:
time: 25.7 us; the launch traced here: 25.6 us
  Pallas kernels  23.9 us (93%)
  local copies, waits for them, and re-layouts  1.62 us (6%)
    pallas_call x1, Pallas kernels, local(): pl.pallas_call(kernel, out_shape=jax.ShapeDtypeStruct(guesses.shape, f32)...  23.9 us
    unnamed x1, local copies, waits for them, and re-layouts  1.62 us

profile of v2, /device:TPU:25, one launch (start us, length us, event | category | flops | bytes accessed | tf_op | source)
XLA Modules:
  0.0 25.6 jit_solution(8140121752039048384)
XLA Ops:
  0.0 23.9 %shard_map.46 = f32[1,128,384]{2,1,0:T(8,128)} custom-call(f32[128,384]{1,0:T(8,128)} %initial.1, f32[1,128,384]{2,1,0:T(8,128)} %guesses.1, f32[128,384]{1,0:T(8,128)} %conduct.1, f32[128,384]{1,0:T(8,128)} %source.1), custom_call_target="tpu_custom_call" | custom-call | tf_op jit(solution)/shard_map/pallas_call | solution.py:555
  24.0 1.6 %copy.6 = f32[1,128,384]{2,1,0:T(8,128)} copy(f32[1,128,384]{2,1,0:T(8,128)} %shard_map.46) | data formatting | bytes 393216

commit v3 on v2

--- a/solution.py
+++ b/solution.py
@@ -16,8 +16,9 @@
 CROWS = ROWS // 2
 T_CHAIN = (CROWS + 32) // 8
 LOW, HIGH = 16, 112
-OWN, FROM_N, FROM_S, FROM_L, FROM_R, FROM_NL, FROM_NR, FROM_SL, FROM_SR, SLOT = 0, 12, 15, 18, 19, 20, 21, 22, 23, 24
-R_N, R_S, R_L, R_R, R_NL, R_NR, R_SL, R_SR, R_ALL = 0, 18, 36, 48, 60, 63, 66, 69, 72
+OWN, FROM_N, FROM_S, FROM_L, FROM_R, SLOT = 0, 12, 15, 18, 19, 21
+FROM_NL, FROM_NR, FROM_SL, FROM_SR = range(4)
+R_N, R_S, R_L, R_R, R_NL, R_NR, R_SL, R_SR, R_ALL = 0, 18, 36, 48, 60, 61, 62, 63, 64
 
 
 def roll(x, shift, axis):
@@ -48,8 +49,7 @@
         east.append(flux(v[W - 1], k[W - 1], roll(v[0], -1, 1), roll(k[0], -1, 1)))
         west = [roll(east[W - 1], 1, 1)] + east[:-1]
         for w in range(W):
-            total = (v[w] + drift[t, w]) + ((east[w] - west[w]) + (below[w] - above[w]))
-            emit(t, w, v[w], total)
+            emit(t, w, v[w], drift[t, w] + ((east[w] - west[w]) + (below[w] - above[w])))
         here, above = following, below
 
 
@@ -61,11 +61,13 @@
             x = x * row_masks[t]
         return x
 
-    def first(t, w, value, total):
-        section[t, w] = keep(t, w, total)
-
-    def second(t, w, value, total):
-        result = keep(t, w, 0.5 * (state[t, w] + total))
+    def first(t, w, value, increment):
+        middle = value + increment
+        state[t, w] = middle
+        section[t, w] = keep(t, w, middle + increment)
+
+    def second(t, w, value, increment):
+        result = keep(t, w, state[t, w] + increment)
         if emit is None:
             state[t, w] = result
         else:
@@ -88,6 +90,12 @@
     return (top + middle) + low
 
 
+def skew(x, step, sublane):
+    moved = [roll(x, step * k, 1) for k in range(4)]
+    i = sublane & 3
+    return jnp.where(i < 2, jnp.where(i == 0, moved[0], moved[1]), jnp.where(i == 2, moved[2], moved[3]))
+
+
 def pack_group(x, own):
     return [jnp.where(own, x[k], roll(x[3], 96 - 32 * k, 1)) for k in range(3)]
 
@@ -99,7 +107,7 @@
 
 def kernel(
     initial, guesses, conduct, source, out,
-    X, Y, SR, SC, R1, V, A, CH, SD, SPREAD, GATHER, PROLONG, RN, RS, RX, RR, BASE, RV, CA, CC, CSD, NAT, SB, EB, NB,
+    X, Y, SR, SC, SK, R1, V, A, CH, SD, SPREAD, GATHER, PROLONG, RN, RS, RX, RR, BASE, RV, CA, CC, CSD, NAT, SB, SE, EB, EE, NB,
     V12, A12, C12, S12, CN, CB, OUT,
     load_sem, store_sem, send1, recv1, send_relaxed, recv_relaxed, send3, recv3, send_coef, send_share, recv_share, ready,
 ):
@@ -118,6 +126,9 @@
     for step in range(1, nt):
         pl.semaphore_signal(barrier, inc=1, device_id=(lax.rem(me + step, nt), row, col), device_id_type=MESH)
 
+    def await_vectors(ref, sem):
+        pltpu.make_async_copy(ref, ref, sem).wait()
+
     @pl.when(me == last)
     def _():
         pltpu.make_async_copy(initial, X.at[0], load_sem).start()
@@ -154,7 +165,7 @@
 
     pltpu.make_async_copy(X, X, load_sem).wait()
 
-    for field, factor in ((0, None), (1, 0.25 * TIME_STEP), (2, TIME_STEP)):
+    for field, factor in ((0, None), (1, 0.125 * TIME_STEP), (2, 0.5 * TIME_STEP)):
         spread = move_columns(X[field], SPREAD[...])
         for w in range(4):
             part = spread[:, 128 * w:128 * w + 128]
@@ -180,16 +191,83 @@
                     slot_of = (q + 12) % 16 if side == 0 else q
                     packed = block if packed is None else jnp.where(eighth == slot_of, block, packed)
                 SC[side, quarter, field] = packed
+    odd_slot = (lane & 4) != 0
+    for side in range(2):
+        for end, quarter in ((0, 0), (1, 3)):
+            fields = [SC[side, quarter, field] for field in range(3)]
+            if side == 1:
+                half = (lane < 64) if end == 0 else (lane >= 64)
+                pair = jnp.where(odd_slot, roll(fields[1], 4, 1), fields[0])
+            else:
+                half = ((lane + 32) & 127) < 64 if end == 0 else ((lane + 32) & 127) >= 64
+                pair = jnp.where(odd_slot, fields[0], roll(fields[1], -4, 1))
+            SK[side, end] = jnp.where(half, pair, roll(fields[2], 64, 1))
+
+    def pack_coarse(which):
+        def block(rb, w):
+            return NAT[which, w, 8 + 8 * rb:16 + 8 * rb, :]
+
+        for g in range(4):
+            packed = pack_group([block(2 * g + i // 2, i % 2) for i in range(4)], own_lanes)
+            for k in range(3):
+                SB[which, 3 * g + k] = packed[k]
+        for side in range(2):
+            packed = None
+            for q in range(16):
+                moved = roll(block(q // 2, q % 2), 8 * q - LOW if side == 0 else 8 * q - (HIGH - 8), 1)
+                packed = moved if packed is None else jnp.where(eighth == q, moved, packed)
+            SB[which, 12 + side] = packed
+            for end in range(2):
+                moved = skew(roll(packed, 32 if end else 0, 1), 32, sublane)
+                moved = jnp.where((lane // 32) == (sublane & 3), moved, 0.0)
+                moved = moved + roll(moved, 1, 0)
+                moved = moved + roll(moved, 2, 0)
+                SE[which, 2 * side + end, 0:1, :] = moved[3:4, :]
+                SE[which, 2 * side + end, 1:2, :] = moved[7:8, :]
+
+    def coarse_copies(which, slot, tm, send, recv):
+        def copy(src, dst, where):
+            return pltpu.make_async_remote_copy(src, dst, send, recv, (tm,) + where, MESH)
+
+        def vectors(a, size, k, where):
+            return copy(SB.at[which, a:a + size], EB.at[slot, k:k + size], where)
+
+        return [
+            copy(SE.at[which, 0], EE.at[slot, FROM_SR], (north, left)),
+            copy(SE.at[which, 2], EE.at[slot, FROM_SL], (north, right)),
+            copy(SE.at[which, 1], EE.at[slot, FROM_NR], (south, left)),
+            copy(SE.at[which, 3], EE.at[slot, FROM_NL], (south, right)),
+            vectors(0, 3, FROM_S, (north, col)),
+            vectors(9, 3, FROM_N, (south, col)),
+            vectors(12, 1, FROM_R, (row, left)),
+            vectors(13, 1, FROM_L, (row, right)),
+            vectors(0, 12, OWN, (row, col)),
+        ]
+
+    coef_copies = [copy for k in (1, 2) for copy in coarse_copies(k, 6 + k, me, send_coef, recv3.at[7])[:8]]
+
+    @pl.when(core == 1)
+    def _():
+        for k in (1, 2):
+            for rb in range(8):
+                for w in range(2):
+                    def at(ww, r):
+                        return Y[k, ww, pl.ds(HALO + 16 * rb + r, 8, stride=2), :]
+                    total = (at(2 * w, 0) + at(2 * w + 1, 0)) + (at(2 * w, 1) + at(2 * w + 1, 1))
+                    NAT[k, w, 8 + 8 * rb:16 + 8 * rb, :] = 0.25 * total if k == 1 else total
+            pack_coarse(k)
+            for v in range(12):
+                EB[6 + k, v] = SB[k, v]
 
     pl.semaphore_wait(barrier, 8 + nt - 1)
 
     first_exchange = [
         pltpu.make_async_remote_copy(s, R1.at[k:k + size], send1, recv1, (me,) + w, MESH)
         for s, k, size, w in [
-            (SC.at[1, 3], R_NL, 3, (south, right)),
-            (SC.at[0, 3], R_NR, 3, (south, left)),
-            (SC.at[1, 0], R_SL, 3, (north, right)),
-            (SC.at[0, 0], R_SR, 3, (north, left)),
+            (SK.at[1, 1:2], R_NL, 1, (south, right)),
+            (SK.at[0, 1:2], R_NR, 1, (south, left)),
+            (SK.at[1, 0:1], R_SL, 1, (north, right)),
+            (SK.at[0, 0:1], R_SR, 1, (north, left)),
             (SR.at[0], R_S, 18, (north, col)),
             (SR.at[1], R_N, 18, (south, col)),
         ]
@@ -200,6 +278,12 @@
                 SC.at[side, quarter], R1.at[k + 3 * quarter:k + 3 * quarter + 3], send1, recv1, (me,) + w, MESH))
     for copy in first_exchange:
         copy.start()
+
+    @pl.when(core == 1)
+    def _():
+        for copy in coef_copies:
+            copy.start()
+
     pltpu.make_async_copy(R1, R1, recv1).wait()
 
     for step in range(1, nt):
@@ -207,7 +291,6 @@
 
     top16, bottom16 = strip_mask(0, at_top), strip_mask(7, at_bottom)
     masks = [in_lanes * (top16 if t < HALO else 1.0) * (bottom16 if t >= T_FINE - HALO else 1.0) for t in range(T_FINE)]
-    odd_slot = (lane & 4) != 0
     for field, dest in ((1, CH), (0, V), (2, SD)):
         halo = {}
         for e in range(EXT // 8):
@@ -219,7 +302,11 @@
                 rb = e - 2
                 l, r = R_L + 3 * (rb // 4), R_R + 3 * (rb // 4)
             if (l, r) not in halo:
-                halo[l, r] = jnp.where(odd_slot, R1[r + field], R1[l + field])
+                if e < 2 or e >= 18:
+                    shift = (0, 4, 64)[field]
+                    halo[l, r] = jnp.where(odd_slot, roll(R1[r], shift, 1), roll(R1[l], -shift, 1))
+                else:
+                    halo[l, r] = jnp.where(odd_slot, R1[r + field], R1[l + field])
             if e < 2 or e >= 18:
                 start = (R_N + e * 3 if e < 2 else R_S + (e - 18) * 3) + field * 6
                 values = unpack_group([R1[start + k] for k in range(3)], lane)
@@ -235,56 +322,10 @@
     def four(ref, t, w):
         return (ref[2 * t, 2 * w] + ref[2 * t, 2 * w + 1]) + (ref[2 * t + 1, 2 * w] + ref[2 * t + 1, 2 * w + 1])
 
-    def pack_coarse(which):
-        def block(rb, w):
-            return NAT[which, w, 8 + 8 * rb:16 + 8 * rb, :]
-
-        for g in range(4):
-            packed = pack_group([block(2 * g + i // 2, i % 2) for i in range(4)], own_lanes)
-            for k in range(3):
-                SB[which, 3 * g + k] = packed[k]
-        for side in range(2):
-            packed = None
-            for q in range(16):
-                moved = roll(block(q // 2, q % 2), 8 * q - LOW if side == 0 else 8 * q - (HIGH - 8), 1)
-                packed = moved if packed is None else jnp.where(eighth == q, moved, packed)
-            SB[which, 12 + side] = packed
-
-    def coarse_copies(which, slot, tm, send, recv):
-        src = SB.at[which]
-        plan = [
-            (12, 1, FROM_SR, (north, left)),
-            (13, 1, FROM_SL, (north, right)),
-            (12, 1, FROM_NR, (south, left)),
-            (13, 1, FROM_NL, (south, right)),
-            (0, 3, FROM_S, (north, col)),
-            (9, 3, FROM_N, (south, col)),
-            (12, 1, FROM_R, (row, left)),
-            (13, 1, FROM_L, (row, right)),
-            (0, 12, OWN, (row, col)),
-        ]
-        return [pltpu.make_async_remote_copy(src.at[a:a + size], EB.at[slot, k:k + size], send, recv, (tm,) + w, MESH)
-                for a, size, k, w in plan]
-
     for t in range(T_COARSE):
         for w in range(2):
-            c, s = 0.25 * four(CH, t, w), four(SD, t, w)
-            CC[t, w] = c
-            CSD[t, w] = s
-            NAT[1, w, pl.ds(t, 8, stride=T_COARSE), :] = c
-            NAT[2, w, pl.ds(t, 8, stride=T_COARSE), :] = s
-
-    coef_copies = [copy for k in (1, 2) for copy in coarse_copies(k, 6 + k, me, send_coef, recv3.at[7])[:8]]
-
-    @pl.when(core == 1)
-    def _():
-        for k in (1, 2):
-            pack_coarse(k)
-        for copy in coef_copies:
-            copy.start()
-        for k in (1, 2):
-            for v in range(12):
-                EB[6 + k, v] = SB[k, v]
+            CC[t, w] = 0.25 * four(CH, t, w)
+            CSD[t, w] = four(SD, t, w)
 
     fine_rows = {HALO - 1: top16, T_FINE - HALO: bottom16}
 
@@ -355,19 +396,23 @@
             copy.start()
 
     def finish(k, copies):
-        size = {8: 12, 9: 24, 1: 12}[len(copies)]
-        whole = EB.at[0, 0:size]
-        pltpu.make_async_copy(whole, whole, send3.at[k]).wait()
+        size = {8: 9, 9: 21, 1: 12}[len(copies)]
+        await_vectors(EB.at[0, 0:size], send3.at[k])
 
     each_receiver(start)
 
     def unpack(slot, store):
         def halo_at(e):
             if e < 2:
-                return EB[slot, FROM_NL], EB[slot, FROM_NR], 6 + e
+                return corners[FROM_NL], corners[FROM_NR], e
             if e >= 10:
-                return EB[slot, FROM_SL], EB[slot, FROM_SR], e - 10
+                return corners[FROM_SL], corners[FROM_SR], e - 10
             return EB[slot, FROM_L], EB[slot, FROM_R], e - 2
+
+        corners = []
+        for k in range(4):
+            two = jnp.where(sublane < 4, EE[slot, k, 0:1, :], EE[slot, k, 1:2, :])
+            corners.append(skew(two, -32, sublane))
 
         for g in range(6):
             base = FROM_N if g == 0 else FROM_S if g == 5 else OWN + 3 * (g - 1)
@@ -388,9 +433,6 @@
             for w in range(2):
                 store(t, w, NB[w, pl.ds(t, 8, stride=T_CHAIN), :])
 
-    def await_vectors(ref, sem):
-        pltpu.make_async_copy(ref, ref, sem).wait()
-
     chain_rows = {15 % T_CHAIN: strip_mask(15 // T_CHAIN, at_top), 80 % T_CHAIN: strip_mask(80 // T_CHAIN, at_bottom)}
     share = pltpu.make_async_remote_copy(
         CB, CN, send_share, recv_share, (jnp.maximum(me - 1, 0), row, col), MESH)
@@ -521,6 +563,7 @@
         vmem((3, 4, EXT, 128), f32),
         vmem((2, 18, 8, 128), f32),
         vmem((2, 4, 3, 8, 128), f32),
+        vmem((2, 2, 8, 128), f32),
         vmem((R_ALL, 8, 128), f32),
         vmem(fine, f32),
         vmem(fine, f32),
@@ -540,7 +583,9 @@
         vmem(coarse, f32),
         vmem((3, 2, EXT // 2, 128), f32),
         vmem((3, 14, 8, 128), f32),
+        vmem((3, 4, 2, 128), f32),
         vmem((9, SLOT, 8, 128), f32),
+        vmem((9, 4, 2, 128), f32),
         vmem((2, CROWS + 32, 128), f32),
         vmem(chain, f32),
         vmem(chain, f32),
@@ -558,7 +603,7 @@
         in_specs=[pl.BlockSpec(memory_space=pl.ANY)] * 4,
         out_specs=pl.BlockSpec(memory_space=pl.ANY),
         scratch_shapes=scratch,
-        compiler_params=pltpu.CompilerParams(collective_id=0, has_side_effects=True, vmem_limit_bytes=60 * 1024 * 1024),
+        compiler_params=pltpu.CompilerParams(collective_id=0, has_side_effects=True, vmem_limit_bytes=54976 * 1024),
     )(initial, guesses, conduct, source)
 
 

time: 25.7 us -> 23.5 us (0.914)
  Pallas kernels: 23.9 us -> 22.7 us
  local copies, waits for them, and re-layouts: 1.62 us -> 0.68 us
    pallas_call x1, Pallas kernels: 23.9 us -> 22.7 us  [local(): pl.pallas_call(kernel, out_shape=jax.ShapeDtypeStruct(guesses.shape, f32)...]
    unnamed x1, local copies, waits for them, and re-layouts: 1.62 us -> 0.68 us
where the time goes in v3:
time: 23.5 us; the launch traced here: 23.3 us
  Pallas kernels  22.7 us (97%)
  local copies, waits for them, and re-layouts  0.68 us (3%)
    pallas_call x1, Pallas kernels, local(): pl.pallas_call(kernel, out_shape=jax.ShapeDtypeStruct(guesses.shape, f32)...  22.7 us
    unnamed x1, local copies, waits for them, and re-layouts  0.68 us

profile of v3, /device:TPU:25, one launch (start us, length us, event | category | flops | bytes accessed | tf_op | source)
XLA Modules:
  0.0 23.3 jit_solution(16781954591631439119)
XLA Ops:
  0.0 22.7 %shard_map.46 = f32[1,128,384]{2,1,0:T(8,128)S(1)} custom-call(f32[128,384]{1,0:T(8,128)} %initial.1, f32[1,128,384]{2,1,0:T(8,128)} %guesses.1, f32[128,384]{1,0:T(8,128)} %conduct.1, f32[128,384]{1,0:T(8,128)} %source.1), custom_call_target="tpu_custom_call" | custom-call | tf_op jit(solution)/shard_map/pallas_call | solution.py:600
  22.7 0.7 %copy.6 = f32[1,128,384]{2,1,0:T(8,128)} copy(f32[1,128,384]{2,1,0:T(8,128)S(1)} %shard_map.46) | data formatting | bytes 393216

commit v4 on v3

--- a/solution.py
+++ b/solution.py
@@ -16,7 +16,7 @@
 CROWS = ROWS // 2
 T_CHAIN = (CROWS + 32) // 8
 LOW, HIGH = 16, 112
-OWN, FROM_N, FROM_S, FROM_L, FROM_R, SLOT = 0, 12, 15, 18, 19, 21
+OWN, FROM_N, FROM_S, FROM_L, FROM_R, SLOT, SHALLOW = 0, 12, 15, 18, 19, 21, 19
 FROM_NL, FROM_NR, FROM_SL, FROM_SR = range(4)
 R_N, R_S, R_L, R_R, R_NL, R_NR, R_SL, R_SR, R_ALL = 0, 18, 36, 48, 60, 61, 62, 63, 64
 
@@ -107,7 +107,7 @@
 
 def kernel(
     initial, guesses, conduct, source, out,
-    X, Y, SR, SC, SK, R1, V, A, CH, SD, SPREAD, GATHER, PROLONG, RN, RS, RX, RR, BASE, RV, CA, CC, CSD, NAT, SB, SE, EB, EE, NB,
+    X, Y, HX, SR, SC, SK, R1, V, A, CH, SD, SPREAD, GATHER, PROLONG, RN, RS, RX, RR, BASE, RV, CA, CC, CSD, NAT, SB, SE, EB, EE, NB,
     V12, A12, C12, S12, CN, CB, OUT,
     load_sem, store_sem, send1, recv1, send_relaxed, recv_relaxed, send3, recv3, send_coef, send_share, recv_share, ready,
 ):
@@ -211,6 +211,9 @@
             packed = pack_group([block(2 * g + i // 2, i % 2) for i in range(4)], own_lanes)
             for k in range(3):
                 SB[which, 3 * g + k] = packed[k]
+        for w in range(2):
+            SB[which, 14 + w] = block(0, w)
+            SB[which, 16 + w] = block(7, w)
         for side in range(2):
             packed = None
             for q in range(16):
@@ -225,7 +228,7 @@
                 SE[which, 2 * side + end, 0:1, :] = moved[3:4, :]
                 SE[which, 2 * side + end, 1:2, :] = moved[7:8, :]
 
-    def coarse_copies(which, slot, tm, send, recv):
+    def coarse_copies(which, slot, tm, send, recv, deep=True):
         def copy(src, dst, where):
             return pltpu.make_async_remote_copy(src, dst, send, recv, (tm,) + where, MESH)
 
@@ -237,8 +240,8 @@
             copy(SE.at[which, 2], EE.at[slot, FROM_SL], (north, right)),
             copy(SE.at[which, 1], EE.at[slot, FROM_NR], (south, left)),
             copy(SE.at[which, 3], EE.at[slot, FROM_NL], (south, right)),
-            vectors(0, 3, FROM_S, (north, col)),
-            vectors(9, 3, FROM_N, (south, col)),
+            vectors(0, 3, FROM_S, (north, col)) if deep else vectors(14, 2, FROM_S, (north, col)),
+            vectors(9, 3, FROM_N, (south, col)) if deep else vectors(16, 2, FROM_N, (south, col)),
             vectors(12, 1, FROM_R, (row, left)),
             vectors(13, 1, FROM_L, (row, right)),
             vectors(0, 12, OWN, (row, col)),
@@ -310,14 +313,14 @@
             if e < 2 or e >= 18:
                 start = (R_N + e * 3 if e < 2 else R_S + (e - 18) * 3) + field * 6
                 values = unpack_group([R1[start + k] for k in range(3)], lane)
-            else:
-                values = [own_block(field, w, rb) for w in range(4)]
+                for w in range(4):
+                    Y[field, w, 8 * e:8 * e + 8, :] = values[w]
+            HX[field, 8 * e:8 * e + 8, :] = roll(halo[l, r], -32 * (rb % 4), 1)
+        for t in range(T_FINE):
+            around = HX[field, pl.ds(t, 8, stride=T_FINE), :]
             for w in range(4):
-                q = (rb % 4) * 4 + w
-                Y[field, w, 8 * e:8 * e + 8, :] = jnp.where(own_lanes, values[w], roll(halo[l, r], LOW - 4 - 8 * q, 1))
-        for t in range(T_FINE):
-            for w in range(4):
-                dest[t, w] = Y[field, w, pl.ds(t, 8, stride=T_FINE), :] * masks[t]
+                value = Y[field, w, pl.ds(t, 8, stride=T_FINE), :]
+                dest[t, w] = jnp.where(own_lanes, value, roll(around, LOW - 4 - 8 * w, 1)) * masks[t]
 
     def four(ref, t, w):
         return (ref[2 * t, 2 * w] + ref[2 * t, 2 * w + 1]) + (ref[2 * t + 1, 2 * w] + ref[2 * t + 1, 2 * w + 1])
@@ -368,40 +371,40 @@
     is_last = me == last
 
     def each_receiver(action):
-        for k in (2, 3, 1, 0):
-            copies = coarse_copies(0, slot_out, 2 * lax.rem(chip + k, chips) + 1, send3.at[k], recv3.at[slot_out])
+        for k in (0, 3, 2, 1):
+            shallow, deep = [
+                coarse_copies(0, slot_out, 2 * lax.rem(chip + k, chips) + 1, send3.at[k], recv3.at[slot_out], deep)
+                for deep in (False, True)]
             if k == 0:
                 @pl.when(is_last)
                 def _():
-                    action(k, copies[:8])
+                    action(k, deep[:8], SLOT - FROM_N)
                 continue
             reached = jnp.logical_or(is_last, jnp.logical_and(chip + k < chips, me < last - 1))
-            tile_only = k == 1
-
-            @pl.when(reached)
+            special = me == 0 if k == 3 else core == 1 if k == 1 else None
+
+            @pl.when(reached if special is None else jnp.logical_and(reached, jnp.logical_not(special)))
             def _():
-                if tile_only:
-                    @pl.when(core == 0)
-                    def _():
-                        action(k, copies)
-
-                    @pl.when(core == 1)
-                    def _():
-                        action(k, copies[8:])
-                else:
-                    action(k, copies)
-
-    def start(k, copies):
+                action(k, shallow, SHALLOW)
+
+            if special is not None:
+                @pl.when(jnp.logical_and(reached, special))
+                def _():
+                    if k == 3:
+                        action(k, deep, SLOT)
+                    else:
+                        action(k, shallow[8:], FROM_N)
+
+    def start(k, copies, vectors):
         for copy in copies:
             copy.start()
 
-    def finish(k, copies):
-        size = {8: 9, 9: 21, 1: 12}[len(copies)]
-        await_vectors(EB.at[0, 0:size], send3.at[k])
+    def finish(k, copies, vectors):
+        await_vectors(EB.at[0, 0:vectors], send3.at[k])
 
     each_receiver(start)
 
-    def unpack(slot, store):
+    def unpack(slot, store, deep=True):
         def halo_at(e):
             if e < 2:
                 return corners[FROM_NL], corners[FROM_NR], e
@@ -416,7 +419,10 @@
 
         for g in range(6):
             base = FROM_N if g == 0 else FROM_S if g == 5 else OWN + 3 * (g - 1)
-            values = unpack_group([EB[slot, base + k] for k in range(3)], lane)
+            three = [EB[slot, base + k] for k in range(3)]
+            values = unpack_group(three, lane)
+            if g in (0, 5):
+                values = [jnp.where(deep, values[i], three[i % 2]) for i in range(4)]
             mask = in_lanes
             if g == 0:
                 mask = mask * jnp.where(at_top, 0.0, 1.0)
@@ -492,9 +498,23 @@
 
         @pl.when(jnp.logical_and(me != last, me > 1))
         def _():
-            await_vectors(EB.at[0], recv3.at[0])
-
-        unpack(0, put)
+            await_vectors(EB.at[0, 0:SHALLOW], recv3.at[0])
+
+        unpack(0, put, is_last)
+
+        @pl.when(me > 1)
+        def _():
+            heun(V12, A12, C12, S12, T_CHAIN, 2, in_lanes, chain_rows)
+
+            @pl.when(is_last)
+            def _():
+                await_vectors(EB.at[1], recv3.at[1])
+
+            @pl.when(jnp.logical_not(is_last))
+            def _():
+                await_vectors(EB.at[1, 0:SHALLOW], recv3.at[1])
+
+            unpack(1, add, is_last)
 
         def body(slot, carry):
             final = slot == me - 1
@@ -507,13 +527,13 @@
 
             @pl.when(jnp.logical_not(final))
             def _():
-                await_vectors(EB.at[slot], recv3.at[slot])
+                await_vectors(EB.at[slot, 0:SHALLOW], recv3.at[slot])
 
             heun(V12, A12, C12, S12, T_CHAIN, 2, in_lanes, chain_rows)
-            unpack(slot, add)
+            unpack(slot, add, False)
             return carry
 
-        lax.fori_loop(1, me, body, 0)
+        lax.fori_loop(2, me, body, 0)
         natural(CN)
 
         @pl.when(me > 1)
@@ -561,6 +581,7 @@
     scratch = [
         vmem((3, ROWS, COLS), f32),
         vmem((3, 4, EXT, 128), f32),
+        vmem((3, EXT, 128), f32),
         vmem((2, 18, 8, 128), f32),
         vmem((2, 4, 3, 8, 128), f32),
         vmem((2, 2, 8, 128), f32),
@@ -582,7 +603,7 @@
         vmem(coarse, f32),
         vmem(coarse, f32),
         vmem((3, 2, EXT // 2, 128), f32),
-        vmem((3, 14, 8, 128), f32),
+        vmem((3, 18, 8, 128), f32),
         vmem((3, 4, 2, 128), f32),
         vmem((9, SLOT, 8, 128), f32),
         vmem((9, 4, 2, 128), f32),

time: 23.5 us -> 23.1 us (0.983)
  Pallas kernels: 22.7 us -> 22.3 us
    pallas_call x1, Pallas kernels: 22.7 us -> 22.3 us  [local(): pl.pallas_call(kernel, out_shape=jax.ShapeDtypeStruct(guesses.shape, f32)...]
where the time goes in v4:
time: 23.1 us; the launch traced here: 23 us
  Pallas kernels  22.3 us (97%)
  local copies, waits for them, and re-layouts  0.68 us (3%)
    pallas_call x1, Pallas kernels, local(): pl.pallas_call(kernel, out_shape=jax.ShapeDtypeStruct(guesses.shape, f32)...  22.3 us
    unnamed x1, local copies, waits for them, and re-layouts  0.68 us

profile of v4, /device:TPU:25, one launch (start us, length us, event | category | flops | bytes accessed | tf_op | source)
XLA Modules:
  0.0 23.0 jit_solution(13005843174174599090)
XLA Ops:
  0.0 22.3 %shard_map.46 = f32[1,128,384]{2,1,0:T(8,128)S(1)} custom-call(f32[128,384]{1,0:T(8,128)} %initial.1, f32[1,128,384]{2,1,0:T(8,128)} %guesses.1, f32[128,384]{1,0:T(8,128)} %conduct.1, f32[128,384]{1,0:T(8,128)} %source.1), custom_call_target="tpu_custom_call" | custom-call | tf_op jit(solution)/shard_map/pallas_call | solution.py:621
  22.3 0.7 %copy.6 = f32[1,128,384]{2,1,0:T(8,128)} copy(f32[1,128,384]{2,1,0:T(8,128)S(1)} %shard_map.46) | data formatting | bytes 393216

commit v5 on v4

--- a/solution.py
+++ b/solution.py
@@ -18,7 +18,7 @@
 LOW, HIGH = 16, 112
 OWN, FROM_N, FROM_S, FROM_L, FROM_R, SLOT, SHALLOW = 0, 12, 15, 18, 19, 21, 19
 FROM_NL, FROM_NR, FROM_SL, FROM_SR = range(4)
-R_N, R_S, R_L, R_R, R_NL, R_NR, R_SL, R_SR, R_ALL = 0, 18, 36, 48, 60, 61, 62, 63, 64
+R_N, R_S, R_NL, R_NR, R_SL, R_SR, R_L, R_R, R_ALL = 0, 18, 36, 37, 38, 39, 40, 52, 64
 
 
 def roll(x, shift, axis):
@@ -86,8 +86,9 @@
 
 
 def move_columns(x, choice):
-    top, middle, low = [jnp.dot(part, choice, preferred_element_type=jnp.float32) for part in pieces(x)]
-    return (top + middle) + low
+    moved = jnp.dot(jnp.concatenate(pieces(x), axis=0), choice, preferred_element_type=jnp.float32)
+    n = x.shape[0]
+    return (moved[:n] + moved[n:2 * n]) + moved[2 * n:]
 
 
 def skew(x, step, sublane):
@@ -109,7 +110,7 @@
     initial, guesses, conduct, source, out,
     X, Y, HX, SR, SC, SK, R1, V, A, CH, SD, SPREAD, GATHER, PROLONG, RN, RS, RX, RR, BASE, RV, CA, CC, CSD, NAT, SB, SE, EB, EE, NB,
     V12, A12, C12, S12, CN, CB, OUT,
-    load_sem, store_sem, send1, recv1, send_relaxed, recv_relaxed, send3, recv3, send_coef, send_share, recv_share, ready,
+    load_sem, send1, recv1, send_relaxed, recv_relaxed, send3, recv3, send_coef, send_share, recv_share, ready,
 ):
     nt, nx, ny = lax.axis_size("tm"), lax.axis_size("sx"), lax.axis_size("sy")
     me, row, col = lax.axis_index("tm"), lax.axis_index("sx"), lax.axis_index("sy")
@@ -121,7 +122,7 @@
                (north, left), (north, right), (south, left), (south, right)]
 
     barrier = pltpu.get_barrier_semaphore()
-    for r, c in spatial:
+    for r, c in reversed(spatial):
         pl.semaphore_signal(barrier, inc=1, device_id=(me, r, c), device_id_type=MESH)
     for step in range(1, nt):
         pl.semaphore_signal(barrier, inc=1, device_id=(lax.rem(me + step, nt), row, col), device_id_type=MESH)
@@ -247,25 +248,10 @@
             vectors(0, 12, OWN, (row, col)),
         ]
 
-    coef_copies = [copy for k in (1, 2) for copy in coarse_copies(k, 6 + k, me, send_coef, recv3.at[7])[:8]]
-
-    @pl.when(core == 1)
-    def _():
-        for k in (1, 2):
-            for rb in range(8):
-                for w in range(2):
-                    def at(ww, r):
-                        return Y[k, ww, pl.ds(HALO + 16 * rb + r, 8, stride=2), :]
-                    total = (at(2 * w, 0) + at(2 * w + 1, 0)) + (at(2 * w, 1) + at(2 * w + 1, 1))
-                    NAT[k, w, 8 + 8 * rb:16 + 8 * rb, :] = 0.25 * total if k == 1 else total
-            pack_coarse(k)
-            for v in range(12):
-                EB[6 + k, v] = SB[k, v]
-
     pl.semaphore_wait(barrier, 8 + nt - 1)
 
     first_exchange = [
-        pltpu.make_async_remote_copy(s, R1.at[k:k + size], send1, recv1, (me,) + w, MESH)
+        pltpu.make_async_remote_copy(s, R1.at[k:k + size], send1, recv1.at[0], (me,) + w, MESH)
         for s, k, size, w in [
             (SK.at[1, 1:2], R_NL, 1, (south, right)),
             (SK.at[0, 1:2], R_NR, 1, (south, left)),
@@ -278,16 +264,34 @@
     for side, k, w in ((1, R_L, (row, right)), (0, R_R, (row, left))):
         for quarter in range(4):
             first_exchange.append(pltpu.make_async_remote_copy(
-                SC.at[side, quarter], R1.at[k + 3 * quarter:k + 3 * quarter + 3], send1, recv1, (me,) + w, MESH))
+                SC.at[side, quarter], R1.at[k + 3 * quarter:k + 3 * quarter + 3], send1, recv1.at[1], (me,) + w, MESH))
     for copy in first_exchange:
         copy.start()
 
+    coef_copies = [copy for k in (1, 2) for copy in coarse_copies(k, 6 + k, me, send_coef, recv3.at[7])[:8]]
+
     @pl.when(core == 1)
     def _():
+        for k in (1, 2):
+            for rb in range(8):
+                for w in range(2):
+                    def at(ww, r):
+                        return Y[k, ww, pl.ds(HALO + 16 * rb + r, 8, stride=2), :]
+                    total = (at(2 * w, 0) + at(2 * w + 1, 0)) + (at(2 * w, 1) + at(2 * w + 1, 1))
+                    NAT[k, w, 8 + 8 * rb:16 + 8 * rb, :] = 0.25 * total if k == 1 else total
+            pack_coarse(k)
+            for v in range(12):
+                EB[6 + k, v] = SB[k, v]
         for copy in coef_copies:
             copy.start()
 
-    pltpu.make_async_copy(R1, R1, recv1).wait()
+    await_vectors(R1.at[R_L:R_ALL], recv1.at[1])
+    for field in range(3):
+        for rb in range(16):
+            l, r = R_L + 3 * (rb // 4) + field, R_R + 3 * (rb // 4) + field
+            around = jnp.where(odd_slot, R1[r], R1[l])
+            HX[field, 8 * rb + HALO:8 * rb + HALO + 8, :] = roll(around, -32 * (rb % 4), 1)
+    await_vectors(R1.at[0:R_L], recv1.at[0])
 
     for step in range(1, nt):
         pl.semaphore_signal(ready, inc=1, device_id=(lax.rem(me + step, nt), row, col), device_id_type=MESH)
@@ -295,27 +299,15 @@
     top16, bottom16 = strip_mask(0, at_top), strip_mask(7, at_bottom)
     masks = [in_lanes * (top16 if t < HALO else 1.0) * (bottom16 if t >= T_FINE - HALO else 1.0) for t in range(T_FINE)]
     for field, dest in ((1, CH), (0, V), (2, SD)):
-        halo = {}
-        for e in range(EXT // 8):
-            if e < 2:
-                l, r, rb = R_NL, R_NR, 14 + e
-            elif e >= 18:
-                l, r, rb = R_SL, R_SR, e - 18
-            else:
-                rb = e - 2
-                l, r = R_L + 3 * (rb // 4), R_R + 3 * (rb // 4)
-            if (l, r) not in halo:
-                if e < 2 or e >= 18:
-                    shift = (0, 4, 64)[field]
-                    halo[l, r] = jnp.where(odd_slot, roll(R1[r], shift, 1), roll(R1[l], -shift, 1))
-                else:
-                    halo[l, r] = jnp.where(odd_slot, R1[r + field], R1[l + field])
-            if e < 2 or e >= 18:
-                start = (R_N + e * 3 if e < 2 else R_S + (e - 18) * 3) + field * 6
-                values = unpack_group([R1[start + k] for k in range(3)], lane)
-                for w in range(4):
-                    Y[field, w, 8 * e:8 * e + 8, :] = values[w]
-            HX[field, 8 * e:8 * e + 8, :] = roll(halo[l, r], -32 * (rb % 4), 1)
+        for e in (0, 1, 18, 19):
+            l, r, rb = (R_NL, R_NR, 14 + e) if e < 2 else (R_SL, R_SR, e - 18)
+            shift = (0, 4, 64)[field]
+            corners = jnp.where(odd_slot, roll(R1[r], shift, 1), roll(R1[l], -shift, 1))
+            start = (R_N + e * 3 if e < 2 else R_S + (e - 18) * 3) + field * 6
+            values = unpack_group([R1[start + k] for k in range(3)], lane)
+            for w in range(4):
+                Y[field, w, 8 * e:8 * e + 8, :] = values[w]
+            HX[field, 8 * e:8 * e + 8, :] = roll(corners, -32 * (rb % 4), 1)
         for t in range(T_FINE):
             around = HX[field, pl.ds(t, 8, stride=T_FINE), :]
             for w in range(4):
@@ -371,7 +363,7 @@
     is_last = me == last
 
     def each_receiver(action):
-        for k in (0, 3, 2, 1):
+        for k in (3, 2, 0, 1):
             shallow, deep = [
                 coarse_copies(0, slot_out, 2 * lax.rem(chip + k, chips) + 1, send3.at[k], recv3.at[slot_out], deep)
                 for deep in (False, True)]
@@ -554,13 +546,12 @@
         [jnp.concatenate([jnp.where(own_lanes, CN[w, pl.ds(t, 8, stride=8), :] - RR[t, w], 0.0) for w in range(2)], axis=1)
          for t in range(8)], axis=0)
     change = move_columns(change, PROLONG[...])
-    for t in range(8):
-        for k in range(3):
+    for k in range(3):
+        for t in range(8):
             for tt in (2 * t, 2 * t + 1):
                 OUT[k, pl.ds(tt, 8, stride=16), :] = (
                     BASE[k, pl.ds(tt, 8, stride=16), :] + change[8 * t:8 * t + 8, 128 * k:128 * k + 128])
-    for k in range(3):
-        pltpu.make_async_copy(OUT.at[k], out.at[0, :, 128 * k:128 * k + 128], store_sem).start()
+        out[0, :, 128 * k:128 * k + 128] = OUT[k]
 
     await_vectors(R1, send1)
 
@@ -570,7 +561,6 @@
 
     relaxed_copy.wait_send()
     each_receiver(finish)
-    await_vectors(OUT, store_sem)
 
 
 def local(initial, guesses, conduct, source):
@@ -615,14 +605,14 @@
         vmem((2, CROWS, 128), f32),
         vmem((2, CROWS, 128), f32),
         vmem((3, ROWS, 128), f32),
-        dma, dma, dma, dma, dma, dma, dma((nt // 2,)), dma((8,)), dma, dma, dma,
+        dma, dma, dma((2,)), dma, dma, dma((nt // 2,)), dma((8,)), dma, dma, dma,
         pltpu.SemaphoreType.REGULAR,
     ]
     return pl.pallas_call(
         kernel,
         out_shape=jax.ShapeDtypeStruct(guesses.shape, f32),
         in_specs=[pl.BlockSpec(memory_space=pl.ANY)] * 4,
-        out_specs=pl.BlockSpec(memory_space=pl.ANY),
+        out_specs=pl.BlockSpec(memory_space=pltpu.VMEM),
         scratch_shapes=scratch,
         compiler_params=pltpu.CompilerParams(collective_id=0, has_side_effects=True, vmem_limit_bytes=54976 * 1024),
     )(initial, guesses, conduct, source)

time: 23.1 us -> 23.2 us (level)
  no operation moved by 1% of the time
where the time goes in v5:
time: 23.2 us; the launch traced here: 23.1 us
  Pallas kernels  22.4 us (97%)
  local copies, waits for them, and re-layouts  0.68 us (3%)
    pallas_call x1, Pallas kernels, local(): pl.pallas_call(kernel, out_shape=jax.ShapeDtypeStruct(guesses.shape, f32)...  22.4 us
    unnamed x1, local copies, waits for them, and re-layouts  0.68 us

profile of v5, /device:TPU:25, one launch (start us, length us, event | category | flops | bytes accessed | tf_op | source)
XLA Modules:
  0.0 23.1 jit_solution(3951440146116007492)
XLA Ops:
  0.0 22.4 %shard_map.46 = f32[1,128,384]{2,1,0:T(8,128)S(1)} custom-call(f32[128,384]{1,0:T(8,128)} %initial.1, f32[1,128,384]{2,1,0:T(8,128)} %guesses.1, f32[128,384]{1,0:T(8,128)} %conduct.1, f32[128,384]{1,0:T(8,128)} %source.1), custom_call_target="tpu_custom_call" | custom-call | tf_op jit(solution)/shard_map/pallas_call | solution.py:611
  22.4 0.7 %copy.6 = f32[1,128,384]{2,1,0:T(8,128)} copy(f32[1,128,384]{2,1,0:T(8,128)S(1)} %shard_map.46) | data formatting | bytes 393216

commit v6 on v4

--- a/solution.py
+++ b/solution.py
@@ -86,8 +86,9 @@
 
 
 def move_columns(x, choice):
-    top, middle, low = [jnp.dot(part, choice, preferred_element_type=jnp.float32) for part in pieces(x)]
-    return (top + middle) + low
+    moved = jnp.dot(jnp.concatenate(pieces(x), axis=0), choice, preferred_element_type=jnp.float32)
+    n = x.shape[0]
+    return (moved[:n] + moved[n:2 * n]) + moved[2 * n:]
 
 
 def skew(x, step, sublane):
@@ -554,12 +555,11 @@
         [jnp.concatenate([jnp.where(own_lanes, CN[w, pl.ds(t, 8, stride=8), :] - RR[t, w], 0.0) for w in range(2)], axis=1)
          for t in range(8)], axis=0)
     change = move_columns(change, PROLONG[...])
-    for t in range(8):
-        for k in range(3):
+    for k in range(3):
+        for t in range(8):
             for tt in (2 * t, 2 * t + 1):
                 OUT[k, pl.ds(tt, 8, stride=16), :] = (
                     BASE[k, pl.ds(tt, 8, stride=16), :] + change[8 * t:8 * t + 8, 128 * k:128 * k + 128])
-    for k in range(3):
         pltpu.make_async_copy(OUT.at[k], out.at[0, :, 128 * k:128 * k + 128], store_sem).start()
 
     await_vectors(R1, send1)

time: 23.1 us -> 23.1 us (level)
  no operation moved by 1% of the time
where the time goes in v6:
time: 23.1 us; the launch traced here: 23 us
  Pallas kernels  22.3 us (97%)
  local copies, waits for them, and re-layouts  0.68 us (3%)
    pallas_call x1, Pallas kernels, local(): pl.pallas_call(kernel, out_shape=jax.ShapeDtypeStruct(guesses.shape, f32)...  22.3 us
    unnamed x1, local copies, waits for them, and re-layouts  0.68 us

profile of v6, /device:TPU:25, one launch (start us, length us, event | category | flops | bytes accessed | tf_op | source)
XLA Modules:
  0.0 23.0 jit_solution(4114563351231955396)
XLA Ops:
  0.0 22.3 %shard_map.46 = f32[1,128,384]{2,1,0:T(8,128)S(1)} custom-call(f32[128,384]{1,0:T(8,128)} %initial.1, f32[1,128,384]{2,1,0:T(8,128)} %guesses.1, f32[128,384]{1,0:T(8,128)} %conduct.1, f32[128,384]{1,0:T(8,128)} %source.1), custom_call_target="tpu_custom_call" | custom-call | tf_op jit(solution)/shard_map/pallas_call | solution.py:621
  22.3 0.7 %copy.6 = f32[1,128,384]{2,1,0:T(8,128)} copy(f32[1,128,384]{2,1,0:T(8,128)S(1)} %shard_map.46) | data formatting | bytes 393216
